TPU v7x, 32 devices: a whole 2x2x4 slice. The times are simulated.
32 devices in a mesh: wide: 8 (over z, y), narrow: 4 (over x, core).
Axes of the slice: x: 2, y: 2, z: 4, core: 2. Of those that a mesh axis runs over, the one named last changes fastest.
Arguments:
- enc_input: bfloat16 [8192, 768], P(('wide', 'narrow')), may hold values from -6 to 6
- dec_input: bfloat16 [4096, 768], P(('wide', 'narrow')), may hold values from -6 to 6
- enc_lengths: int32 [64], P(('wide', 'narrow')), may hold values from 32 to 192, as said below
- dec_lengths: int32 [64], P(('wide', 'narrow')), may hold values from 16 to 96, as said below
- enc_attn_gain: bfloat16 [768], P(('wide', 'narrow')), may hold values from 0.25 to 1.75
- enc_qkv: bfloat16 [768, 2304], P(('wide', 'narrow')), may hold values from -0.21875 to 0.21875
- enc_attn_out: bfloat16 [768, 768], P(('wide', 'narrow')), may hold values from -1.75 to 1.75
- enc_mlp_gain: bfloat16 [768], P(('wide', 'narrow')), may hold values from 0.25 to 1.75
- enc_mlp_in: bfloat16 [768, 4096], P(('wide', 'narrow')), may hold values from -0.21875 to 0.21875
- enc_mlp_out: bfloat16 [2048, 768], P(('wide', 'narrow')), may hold values from -0.125 to 0.125
- dec_self_gain: bfloat16 [768], P(('wide', 'narrow')), may hold values from 0.25 to 1.75
- dec_qkv: bfloat16 [768, 2304], P(('wide', 'narrow')), may hold values from -0.21875 to 0.21875
- dec_self_out: bfloat16 [768, 768], P(('wide', 'narrow')), may hold values from -1.75 to 1.75
- cross_gain: bfloat16 [768], P(('wide', 'narrow')), may hold values from 0.25 to 1.75
- memory_gain: bfloat16 [768], P(('wide', 'narrow')), may hold values from 0.25 to 1.75
- cross_query: bfloat16 [768, 768], P(('wide', 'narrow')), may hold values from -0.21875 to 0.21875
- cross_kv: bfloat16 [768, 1536], P(('wide', 'narrow')), may hold values from -0.21875 to 0.21875
- cross_out: bfloat16 [768, 768], P(('wide', 'narrow')), may hold values from -1.75 to 1.75
- dec_mlp_gain: bfloat16 [768], P(('wide', 'narrow')), may hold values from 0.25 to 1.75
- dec_mlp_in: bfloat16 [768, 4096], P(('wide', 'narrow')), may hold values from -0.21875 to 0.21875
- dec_mlp_out: bfloat16 [2048, 768], P(('wide', 'narrow')), may hold values from -0.125 to 0.125
- enc_cotangent: bfloat16 [8192, 768], P(('wide', 'narrow')), may hold values from -6 to 6
- dec_cotangent: bfloat16 [4096, 768], P(('wide', 'narrow')), may hold values from -6 to 6
Outputs:
- enc_output: bfloat16 [8192, 768], P(('wide', 'narrow'))
- dec_output: bfloat16 [4096, 768], P(('wide', 'narrow'))
- enc_input_grad: float32 [8192, 768], P(('wide', 'narrow'))
- dec_input_grad: float32 [4096, 768], P(('wide', 'narrow'))
- grad_enc_attn_gain: float32 [768], P(('wide', 'narrow'))
- grad_enc_qkv: float32 [768, 2304], P(('wide', 'narrow'))
- grad_enc_attn_out: float32 [768, 768], P(('wide', 'narrow'))
- grad_enc_mlp_gain: float32 [768], P(('wide', 'narrow'))
- grad_enc_mlp_in: float32 [768, 4096], P(('wide', 'narrow'))
- grad_enc_mlp_out: float32 [2048, 768], P(('wide', 'narrow'))
- grad_dec_self_gain: float32 [768], P(('wide', 'narrow'))
- grad_dec_qkv: float32 [768, 2304], P(('wide', 'narrow'))
- grad_dec_self_out: float32 [768, 768], P(('wide', 'narrow'))
- grad_cross_gain: float32 [768], P(('wide', 'narrow'))
- grad_memory_gain: float32 [768], P(('wide', 'narrow'))
- grad_cross_query: float32 [768, 768], P(('wide', 'narrow'))
- grad_cross_kv: float32 [768, 1536], P(('wide', 'narrow'))
- grad_cross_out: float32 [768, 768], P(('wide', 'narrow'))
- grad_dec_mlp_gain: float32 [768], P(('wide', 'narrow'))
- grad_dec_mlp_in: float32 [768, 4096], P(('wide', 'narrow'))
- grad_dec_mlp_out: float32 [2048, 768], P(('wide', 'narrow'))
Inputs may be any that keep to these rules, and one draw needn't show every extreme that they name: `enc_lengths`: the 2 patch counts of one device sum to at most 256; some item has exactly 192 patches. `dec_lengths`: the 2 table lengths of one device sum to at most 128; some item has exactly 96 tokens.
All inputs are finite; a program needn't handle non-finite values.
Results may differ from a plain program's by a relative error of at most 0.02.
Values may be sent and summed in bfloat16 or wider, within the bound.
A program may use at most 320 MiB of HBM per device.

v0:
```python
import functools

import jax
import jax.numpy as jnp
from jax import lax
from jax.experimental import pallas as pl
from jax.experimental.pallas import tpu as pltpu
from jax.sharding import PartitionSpec as P

D = 768
HEADS = 12
HEAD_DIM = 64
AXES = ("wide", "narrow")
MESH = pl.DeviceIdType.MESH

Z = 4
PIECES = (
    (11, 0, 768, False),
    (0, 0, 1152, False), (0, 1152, 1152, False), (1, 0, 768, True),
    (2, 0, 2048, False), (2, 2048, 2048, True), (3, 0, 768, False),
    (4, 0, 1152, False), (4, 1152, 1152, True), (5, 0, 768, False), (6, 0, 768, False),
    (7, 0, 1536, True), (8, 0, 768, False),
    (9, 0, 2048, False), (9, 2048, 2048, True), (10, 0, 768, False),
)


class Place:
    def __init__(self):
        self.w, self.n = lax.axis_index("wide"), lax.axis_index("narrow")
        self.z, self.y = self.w // 2, self.w % 2
        self.x, self.c = self.n // 2, self.n % 2
        w, n, y, x, c = self.w, self.n, self.y, self.x, self.c
        self.sibling = (w, n + 1 - 2 * c)
        self.first = (w + (1 - c) * (1 - 2 * y), n + c * (2 - 4 * x))
        self.last = (w + c * (1 - 2 * y), n + (1 - c) * (2 - 4 * x))
        self.above = (w + 2, n)
        self.below = (w - 2, n)

    def barrier(self):
        sem = pltpu.get_barrier_semaphore()
        for device in (self.sibling, self.first, self.last):
            pl.semaphore_signal(sem, inc=1, device_id=device, device_id_type=MESH)

        @pl.when(self.z < Z - 1)
        def _():
            pl.semaphore_signal(sem, inc=1, device_id=self.above, device_id_type=MESH)

        @pl.when(self.z > 0)
        def _():
            pl.semaphore_signal(sem, inc=1, device_id=self.below, device_id_type=MESH)

        inner = jnp.where(self.z * (Z - 1 - self.z) > 0, 1, 0)
        pl.semaphore_wait(sem, 4 + inner)

    def by_core(self, do):
        @pl.when(self.c == 0)
        def _():
            do(0)

        @pl.when(self.c == 1)
        def _():
            do(1)


def remote(src, dst, sems, index, device):
    send, recv = sems
    return pltpu.make_async_remote_copy(
        src_ref=src, dst_ref=dst, send_sem=send.at[index], recv_sem=recv.at[index],
        device_id=device, device_id_type=MESH,
    )


class Gather:
    PHASES = 7
    SEMS = 10

    def __init__(self, place, part, whole, columns, z_first, sems, base, local_sem):
        self.p, self.z_first, self.sems, self.base = place, z_first, sems, base
        self.part = part.at[:, :, columns]
        self.whole = whole.at[:, :, :, :, :, :, columns]
        self.local = pltpu.make_async_copy(self.part, self.own(), local_sem)

    def own(self):
        p = self.p
        return self.whole.at[p.z, p.y, p.x, p.c]

    def copy(self, src, dst, slot, device):
        return remote(src, dst, self.sems, self.base + slot, device)

    def layer(self, zz, core):
        p = self.p
        if self.z_first:
            return self.whole.at[zz, p.y, p.x, core]
        return self.whole.at[zz, :, p.x, 0] if core == 0 else self.whole.at[zz, p.y, :, 1]

    def half(self, core, mine):
        p = self.p
        if core == 0:
            return self.whole.at[:, :, p.x if mine else 1 - p.x, 0]
        return self.whole.at[:, p.y if mine else 1 - p.y, :, 1]

    def along_z(self, step, sending):
        p = self.p

        def go(core):
            for up in (True, False):
                if sending:
                    zz = p.z - step if up else p.z + step
                    there = (p.z < Z - 1) & (zz >= 0) if up else (p.z > 0) & (zz < Z)
                else:
                    zz = p.z - 1 - step if up else p.z + 1 + step
                    there = zz >= 0 if up else zz < Z

                target = (p.above if up else p.below) if sending else p.last

                @pl.when(there)
                def _():
                    block = self.layer(zz, core)
                    copy = self.copy(block, block, 1 + step * 2 + up, target)
                    copy.start() if sending else copy.wait_recv()

        p.by_core(go)

    def along_z_sent(self):
        p = self.p

        def go(core):
            for step in range(3):
                for up in (True, False):
                    zz = p.z - step if up else p.z + step
                    there = (p.z < Z - 1) & (zz >= 0) if up else (p.z > 0) & (zz < Z)

                    @pl.when(there)
                    def _():
                        block = self.layer(zz, core)
                        self.copy(block, block, 1 + step * 2 + up, p.last).wait_send()

        p.by_core(go)

    def first(self, core):
        p = self.p
        if not self.z_first:
            return self.copy(self.part, self.own(), 0, p.first)
        block = self.whole.at[:, p.y, p.x, core]
        return self.copy(block, block, 0, p.first)

    def last(self, core):
        block = self.half(core, True)
        return self.copy(block, block, 7, self.p.last)

    def across(self, core, mine):
        block = self.half(core, mine)
        return self.copy(block, block, 8 if mine else 9, self.p.sibling)

    def each(self, make, *verbs):
        def go(core):
            copy = make(core)
            for verb in verbs:
                getattr(copy, verb)()

        self.p.by_core(go)

    def phase(self, number):
        early = not self.z_first
        if number == 0:
            self.local.start()
            if early:
                self.each(self.first, "start")
            self.local.wait()
            if not early:
                self.along_z(0, True)
        elif number == 1:
            if early:
                self.each(self.first, "wait_recv")
                self.along_z(0, True)
            else:
                self.along_z(0, False)
                self.along_z(1, True)
        elif number == 2:
            self.along_z(0 if early else 1, False)
            self.along_z(1 if early else 2, True)
        elif number == 3:
            self.along_z(1 if early else 2, False)
            if early:
                self.along_z(2, True)
            else:
                self.each(self.first, "start")
        elif number == 4:
            if early:
                self.along_z(2, False)
            else:
                self.each(self.first, "wait_recv")
            self.each(self.last, "start")
            self.each(lambda core: self.across(core, True), "start")
        elif number == 5:
            self.each(self.last, "wait_recv")
            self.each(lambda core: self.across(core, False), "start")
        else:
            for core in (0, 1):
                @pl.when(self.p.c == core)
                def _():
                    for mine in (True, False):
                        self.across(1 - core, mine).wait_recv()
                        self.across(core, mine).wait_send()
                    self.first(core).wait_send()
                    self.last(core).wait_send()
            self.along_z_sent()


class Scatter:
    PHASES = 8
    SEMS = 9

    def __init__(self, place, parts, columns, z_first, out, total, mine, lasts, zs, firsts, sems, base, local_sem):
        self.p, self.z_first, self.sems, self.base = place, z_first, sems, base
        self.parts = parts.at[:, :, :, :, :, :, columns]
        self.out = out.at[:, :, columns]
        self.total, self.mine, self.lasts, self.zs, self.firsts = total, mine, lasts, zs, firsts
        self.local_sem = local_sem

    def copy(self, src, dst, slot, device):
        return remote(src, dst, self.sems, self.base + slot, device)

    def spot(self, core, last, first=None):
        every = slice(None)
        if first is None:
            return (every, last) if core else (every, every, last)
        return (last, first) if core else (first, last)

    def place_of(self, core):
        p = self.p
        return (p.y, p.x) if core else (p.x, p.y)

    def across(self, core):
        return self.copy(self.parts.at[:, :, :, 1 - core], self.total, 0, self.p.sibling)

    def take(self, core):
        return pltpu.make_async_copy(self.parts.at[:, :, :, core], self.mine, self.local_sem)

    def last(self, core):
        last, _ = self.place_of(core)
        return self.copy(self.total.at[self.spot(core, 1 - last)], self.lasts, 1, self.p.last)

    def first(self, core):
        p = self.p
        last, first = self.place_of(core)
        if self.z_first:
            src = self.total.at[(slice(None), *self.spot(core, last, 1 - first))]
        else:
            src = self.total.at[(p.z, *self.spot(core, last, 1 - first))]
        return self.copy(src, self.firsts, 2, p.first)

    def layer(self, zz, core):
        last, first = self.place_of(core)
        if self.z_first:
            return self.total.at[(zz, *self.spot(core, last, first))]
        return self.total.at[(zz, *self.spot(core, last)[1:])]

    def way(self, step, up, sending):
        z, far = self.p.z, 2 - step
        if sending:
            zz = z + 1 + far if up else z - 1 - far
            return zz, zz < Z if up else zz >= 0
        zz = z + far if up else z - far
        return zz, (z > 0) & (zz < Z) if up else (z < Z - 1) & (zz >= 0)

    def along_z(self, step, verb):
        p = self.p

        def go(core):
            for up in (True, False):
                zz, there = self.way(step, up, verb != "wait_recv")
                target = (p.above if up else p.below) if verb == "start" else p.last

                @pl.when(there)
                def _():
                    copy = self.copy(self.layer(zz, core), self.zs.at[step, int(up)], 3 + step * 2 + up, target)
                    getattr(copy, verb)()

        p.by_core(go)

    def add_z(self, step):
        p = self.p
        for up in (True, False):
            zz, there = self.way(step, up, False)

            @pl.when(there)
            def _():
                arrived = self.zs.at[step, int(up)]
                if self.z_first:
                    self.total[zz, p.y, p.x] += arrived[...]
                else:
                    for k in range(2):
                        self.total[(zz, *self.pair(k))] += arrived[k]

    def pair(self, k):
        p = self.p
        return k * (1 - p.c) + p.y * p.c, p.x * (1 - p.c) + k * p.c

    def each(self, make, *verbs):
        def go(core):
            copy = make(core)
            for verb in verbs:
                getattr(copy, verb)()

        self.p.by_core(go)

    def phase(self, number):
        p, early = self.p, self.z_first
        if number == 0:
            self.each(self.take, "start")
            self.each(self.across, "start")
        elif number == 1:
            self.each(self.take, "wait")
            self.each(self.across, "wait_recv")

            @pl.loop(0, 16)
            def _(i):
                self.total[i // 4, i // 2 % 2, i % 2] += self.mine[i // 4, i // 2 % 2, i % 2]

            self.each(self.last, "start")
        elif number == 2:
            self.each(self.last, "wait_recv")

            @pl.loop(0, 8)
            def _(i):
                self.total[(i // 2, *self.pair(i % 2))] += self.lasts[i // 2, i % 2]

            if early:
                self.each(self.first, "start")
            else:
                self.along_z(0, "start")
        elif number == 3:
            if early:
                self.each(self.first, "wait_recv")

                @pl.loop(0, Z)
                def _(i):
                    self.total[i, p.y, p.x] += self.firsts[i]

                self.along_z(0, "start")
            else:
                self.along_z(0, "wait_recv")
                self.add_z(0)
                self.along_z(1, "start")
        elif number == 4:
            step = 0 if early else 1
            self.along_z(step, "wait_recv")
            self.add_z(step)
            self.along_z(step + 1, "start")
        elif number == 5:
            step = 1 if early else 2
            self.along_z(step, "wait_recv")
            self.add_z(step)
            if early:
                self.along_z(2, "start")
            else:
                self.each(self.first, "start")
        elif number == 6:
            if early:
                self.along_z(2, "wait_recv")
                self.add_z(2)
                self.out[...] = self.total[p.z, p.y, p.x].astype(jnp.float32)
            else:
                self.each(self.first, "wait_recv")
                self.out[...] = self.total[p.z, p.y, p.x].astype(jnp.float32) + self.firsts[...].astype(jnp.float32)
        else:
            for make in (self.across, self.last, self.first):
                self.each(make, "wait_send")
            for step in range(3):
                self.along_z(step, "wait_send")


def gather_body(pieces, count, *refs):
    parts, wholes = refs[:count], refs[count : 2 * count]
    send, recv, local = refs[2 * count :]
    place = Place()
    place.barrier()
    work = [
        Gather(place, parts[m], wholes[m], pl.ds(start, size), z_first, (send, recv), k * Gather.SEMS, local.at[k])
        for k, (m, start, size, z_first) in enumerate(pieces)
    ]
    for slot in range(len(work) + Gather.PHASES - 1):
        for k in range(max(0, slot - Gather.PHASES + 1), min(slot, len(work) - 1) + 1):
            work[k].phase(slot - k)


def gather_all(shards):
    count = len(shards)
    parts = [s.reshape(s.shape[0] // 8, 8, s.shape[1]) for s in shards]
    shapes = [jax.ShapeDtypeStruct((Z, 2, 2, 2, *p.shape), p.dtype) for p in parts]
    sems = len(PIECES) * Gather.SEMS
    wholes = pl.pallas_call(
        functools.partial(gather_body, PIECES, count),
        out_shape=shapes,
        in_specs=[pl.BlockSpec(memory_space=pl.ANY)] * count,
        out_specs=[pl.BlockSpec(memory_space=pl.ANY)] * count,
        scratch_shapes=[
            pltpu.SemaphoreType.DMA((sems,)),
            pltpu.SemaphoreType.DMA((sems,)),
            pltpu.SemaphoreType.DMA((len(PIECES),)),
        ],
        compiler_params=pltpu.CompilerParams(collective_id=0, has_side_effects=True),
    )(*parts)
    return [w.reshape(-1, w.shape[-1]) for w in wholes]


def scatter_body(pieces, count, stages, *refs):
    sums, outs = refs[:count], refs[count : 2 * count]
    scratch = list(refs[2 * count :])
    send, recv, local = scratch[:3]
    scratch = scratch[3:]
    mines = {shape: scratch.pop(0) for shape in stages}
    place = Place()
    place.barrier()
    work = []
    for k, (m, start, size, z_first) in enumerate(pieces):
        total, lasts, zs, firsts = (scratch.pop(0) for _ in range(4))
        mine = mines[(sums[m].shape[4], size)]
        work.append(
            Scatter(
                place, sums[m], pl.ds(start, size), z_first, outs[m], total, mine, lasts, zs, firsts,
                (send, recv), k * Scatter.SEMS, local.at[k],
            )
        )
    for slot in range(len(work) + Scatter.PHASES - 1):
        for k in range(max(0, slot - Scatter.PHASES + 1), min(slot, len(work) - 1) + 1):
            work[k].phase(slot - k)


def scatter_all(sums):
    count = len(sums)
    pieces = PIECES[:0:-1]
    parts = [s.reshape(Z, 2, 2, 2, -1, 8, s.shape[1]) for s in sums]
    groups = [p.shape[4] for p in parts]
    stages = sorted({(groups[m], size) for m, _, size, _ in pieces})
    sems = len(pieces) * Scatter.SEMS
    scratch = [
        pltpu.SemaphoreType.DMA((sems,)),
        pltpu.SemaphoreType.DMA((sems,)),
        pltpu.SemaphoreType.DMA((len(pieces),)),
    ]
    scratch += [pltpu.VMEM((Z, 2, 2, r, 8, size), jnp.bfloat16) for r, size in stages]
    for m, _, size, z_first in pieces:
        block = (groups[m], 8, size)
        scratch += [
            pltpu.VMEM((Z, 2, 2, *block), jnp.bfloat16),
            pltpu.VMEM((Z, 2, *block), jnp.bfloat16),
            pltpu.VMEM((3, 2, *(() if z_first else (2,)), *block), jnp.bfloat16),
            pltpu.VMEM((*((Z,) if z_first else ()), *block), jnp.bfloat16),
        ]
    outs = pl.pallas_call(
        functools.partial(scatter_body, pieces, count, stages),
        out_shape=[jax.ShapeDtypeStruct(p.shape[4:], jnp.float32) for p in parts],
        in_specs=[pl.BlockSpec(memory_space=pl.ANY)] * count,
        out_specs=[pl.BlockSpec(memory_space=pltpu.VMEM)] * count,
        scratch_shapes=scratch,
        compiler_params=pltpu.CompilerParams(
            collective_id=1, has_side_effects=True, vmem_limit_bytes=60 * 2**20
        ),
    )(*parts)
    return [o.reshape(-1, o.shape[-1]) for o in outs]


epsilon = 1e-06
masked_value = -1000000000.0


def norm_rows(values, scales):
    return values * lax.rsqrt(jnp.mean(values * values, axis=-1, keepdims=True) + epsilon) * scales


def norm_back(inputs, scales, grad):
    return jax.vjp(lambda v: norm_rows(v, scales), inputs)[1](grad)[0]


def gated_units(united):
    halfway = united.shape[-1] // 2
    return jax.nn.gelu(united[:, :halfway], approximate=True) * united[:, halfway:]


def row_items(lengths, row_count):
    places = jnp.arange(row_count, dtype=jnp.int32)
    count = lengths.shape[0]
    item, boundary = jnp.zeros((row_count,), jnp.int32), jnp.int32(0)
    for k in range(count):
        boundary = boundary + lengths[k]
        item = item + (places >= boundary).astype(jnp.int32)
    return item


def head_split(matrix):
    return matrix.reshape(matrix.shape[0], HEADS, HEAD_DIM)


def outer_rows(left, right):
    return jnp.einsum("rd,re->de", left, right, preferred_element_type=jnp.float32).astype(jnp.bfloat16)


def back_rows(incoming, matrix):
    return jnp.einsum("re,de->rd", incoming, matrix, preferred_element_type=jnp.float32)


def score_rows(query_heads, key_heads, allowed):
    raw_scores = jnp.einsum(
        "qhd,khd->hqk", query_heads, key_heads, preferred_element_type=jnp.float32
    )
    return jnp.where(allowed[None], raw_scores * HEAD_DIM ** (-0.5), masked_value)


def attend_forward(queries, keys_in, values_in, allowed):
    scores = score_rows(head_split(queries), head_split(keys_in), allowed)
    largest = jnp.max(scores, axis=2, keepdims=True)
    expanded = jnp.exp(scores - largest)
    totals = jnp.sum(expanded, axis=2, keepdims=True)
    weights = (expanded / totals).astype(jnp.bfloat16)
    mixed = jnp.einsum(
        "hqk,khd->qhd", weights, head_split(values_in), preferred_element_type=jnp.float32
    )
    return (mixed.reshape(queries.shape[0], D), largest + jnp.log(totals))


def attend_backward(queries, keys_in, values_in, allowed, log_totals, grad_mixed):
    query_heads = head_split(queries)
    key_heads = head_split(keys_in)
    value_heads = head_split(values_in)
    probs = jnp.exp(score_rows(query_heads, key_heads, allowed) - log_totals)
    grad_heads = head_split(grad_mixed)
    grad_values = jnp.einsum(
        "hqk,qhd->khd", probs.astype(jnp.bfloat16), grad_heads, preferred_element_type=jnp.float32
    )
    grad_probs = jnp.einsum(
        "qhd,khd->hqk", grad_heads, value_heads, preferred_element_type=jnp.float32
    )
    centred = grad_probs - jnp.sum(probs * grad_probs, axis=2, keepdims=True)
    grad_scores = (probs * centred * HEAD_DIM ** (-0.5)).astype(jnp.bfloat16)
    grad_queries = jnp.einsum(
        "hqk,khd->qhd", grad_scores, key_heads, preferred_element_type=jnp.float32
    )
    grad_keys = jnp.einsum(
        "hqk,qhd->khd", grad_scores, query_heads, preferred_element_type=jnp.float32
    )
    return (
        grad_queries.reshape(queries.shape[0], D),
        grad_keys.reshape(keys_in.shape[0], D),
        grad_values.reshape(keys_in.shape[0], D),
    )


def self_forward(inputs, params, allowed, live_rows):
    scales, joined, outward = params
    normed = norm_rows(inputs, scales).astype(jnp.bfloat16)
    projected = jnp.dot(normed, joined, preferred_element_type=jnp.float32).astype(jnp.bfloat16)
    mixed, log_totals = attend_forward(
        projected[:, :D], projected[:, D : 2 * D], projected[:, 2 * D :], allowed
    )
    mixed_low = mixed.astype(jnp.bfloat16)
    branch = jnp.dot(mixed_low, outward, preferred_element_type=jnp.float32)
    return (inputs + live_rows[:, None] * branch, (normed, projected, mixed_low, log_totals))


def self_backward(inputs, params, allowed, live_rows, stored, incoming):
    scales, joined, outward = params
    normed, projected, mixed_low, log_totals = stored
    grad_branch = (live_rows[:, None] * incoming).astype(jnp.bfloat16)
    grad_outward = outer_rows(mixed_low, grad_branch)
    grad_mixed = back_rows(grad_branch, outward).astype(jnp.bfloat16)
    grad_parts = attend_backward(
        projected[:, :D],
        projected[:, D : 2 * D],
        projected[:, 2 * D :],
        allowed,
        log_totals,
        grad_mixed,
    )
    grad_projected = jnp.concatenate(grad_parts, axis=1).astype(jnp.bfloat16)
    grad_joined = outer_rows(normed, grad_projected)
    grad_inputs = norm_back(inputs, scales, back_rows(grad_projected, joined))
    return (incoming + grad_inputs, (grad_joined, grad_outward))


def cross_forward(inputs, memory, params, allowed, live_rows):
    scales, memory_scales, query_map, pair_map, outward = params
    normed = norm_rows(inputs, scales).astype(jnp.bfloat16)
    memory_normed = norm_rows(memory, memory_scales).astype(jnp.bfloat16)
    queries = jnp.dot(normed, query_map, preferred_element_type=jnp.float32).astype(jnp.bfloat16)
    pairs = jnp.dot(memory_normed, pair_map, preferred_element_type=jnp.float32).astype(
        jnp.bfloat16
    )
    mixed, log_totals = attend_forward(queries, pairs[:, :D], pairs[:, D:], allowed)
    mixed_low = mixed.astype(jnp.bfloat16)
    branch = jnp.dot(mixed_low, outward, preferred_element_type=jnp.float32)
    return (
        inputs + live_rows[:, None] * branch,
        (normed, memory_normed, queries, pairs, mixed_low, log_totals),
    )


def cross_backward(inputs, memory, params, allowed, live_rows, stored, incoming):
    scales, memory_scales, query_map, pair_map, outward = params
    normed, memory_normed, queries, pairs, mixed_low, log_totals = stored
    grad_branch = (live_rows[:, None] * incoming).astype(jnp.bfloat16)
    grad_outward = outer_rows(mixed_low, grad_branch)
    grad_mixed = back_rows(grad_branch, outward).astype(jnp.bfloat16)
    grad_queries, grad_keys, grad_values = attend_backward(
        queries, pairs[:, :D], pairs[:, D:], allowed, log_totals, grad_mixed
    )
    grad_queries_low = grad_queries.astype(jnp.bfloat16)
    grad_pairs = jnp.concatenate([grad_keys, grad_values], axis=1).astype(jnp.bfloat16)
    grad_query_map = outer_rows(normed, grad_queries_low)
    grad_pair_map = outer_rows(memory_normed, grad_pairs)
    grad_inputs = norm_back(inputs, scales, back_rows(grad_queries_low, query_map))
    grad_memory = norm_back(memory, memory_scales, back_rows(grad_pairs, pair_map))
    return (
        incoming + grad_inputs,
        grad_memory,
        (grad_query_map, grad_pair_map, grad_outward),
    )


def mlp_forward(inputs, params, live_rows):
    scales, inward, outward = params
    normed = norm_rows(inputs, scales).astype(jnp.bfloat16)
    united = jnp.dot(normed, inward, preferred_element_type=jnp.float32)
    activated = gated_units(united).astype(jnp.bfloat16)
    branch = jnp.dot(activated, outward, preferred_element_type=jnp.float32)
    return (inputs + live_rows[:, None] * branch, (normed, united, activated))


def mlp_backward(inputs, params, live_rows, stored, incoming):
    scales, inward, outward = params
    normed, united, activated = stored
    grad_branch = (live_rows[:, None] * incoming).astype(jnp.bfloat16)
    grad_outward = outer_rows(activated, grad_branch)
    grad_activated = back_rows(grad_branch, outward)
    _, pullback = jax.vjp(gated_units, united)
    grad_united = pullback(grad_activated)[0].astype(jnp.bfloat16)
    grad_inward = outer_rows(normed, grad_united)
    grad_inputs = norm_back(inputs, scales, back_rows(grad_united, inward))
    return (incoming + grad_inputs, (grad_inward, grad_outward))


def plain_gather(shards):
    return [lax.all_gather(s, AXES, axis=0, tiled=True) for s in shards]


def plain_scatter(sums):
    return [lax.psum_scatter(s.astype(jnp.float32), AXES, scatter_dimension=0, tiled=True) for s in sums]


SCALE_OF = (0, None, 1, None, 2, None, 3, 4, None, 5, None)


def per_device(
    linked,
    enc_input,
    dec_input,
    enc_lengths,
    dec_lengths,
    enc_attn_gain,
    enc_qkv,
    enc_attn_out,
    enc_mlp_gain,
    enc_mlp_in,
    enc_mlp_out,
    dec_self_gain,
    dec_qkv,
    dec_self_out,
    cross_gain,
    memory_gain,
    cross_query,
    cross_kv,
    cross_out,
    dec_mlp_gain,
    dec_mlp_in,
    dec_mlp_out,
    enc_cotangent,
    dec_cotangent,
):
    item_count = enc_lengths.shape[0]
    enc_items = row_items(enc_lengths, enc_input.shape[0])
    dec_items = row_items(dec_lengths, dec_input.shape[0])
    enc_live = (enc_items < item_count).astype(jnp.float32)
    dec_live = (dec_items < item_count).astype(jnp.float32)
    enc_padded = enc_items[:, None] == item_count
    dec_padded = dec_items[:, None] == item_count
    enc_allowed = (enc_items[:, None] == enc_items[None, :]) | enc_padded
    dec_places = jnp.arange(dec_input.shape[0], dtype=jnp.int32)
    self_allowed = (dec_items[:, None] == dec_items[None, :]) & (
        dec_places[None, :] <= dec_places[:, None]
    ) | dec_padded
    cross_allowed = (dec_items[:, None] == enc_items[None, :]) | dec_padded
    scales = [
        g.astype(jnp.float32)
        for g in (enc_attn_gain, enc_mlp_gain, dec_self_gain, cross_gain, memory_gain, dec_mlp_gain)
    ]
    shards = (
        enc_qkv, enc_attn_out, enc_mlp_in, enc_mlp_out, dec_qkv, dec_self_out,
        cross_query, cross_kv, cross_out, dec_mlp_in, dec_mlp_out,
    )
    if linked:
        mine = lax.axis_index("wide") * lax.axis_size("narrow") + lax.axis_index("narrow")
        columns = jnp.arange(D, dtype=jnp.int32) // scales[0].shape[0] == mine
        rows = [jnp.where(columns, jnp.tile(g, D // g.shape[0]), 0.0) for g in scales]
        rows += [jnp.zeros((D,), jnp.float32)] * (8 - len(rows))
        *whole, spread = gather_all((*shards, jnp.stack(rows).astype(jnp.bfloat16)))
        gains = jnp.sum(spread.reshape(-1, 8, D).astype(jnp.float32), axis=0)
    else:
        whole = plain_gather(shards)
        gains = plain_gather(scales)
    encoder_start = enc_input.astype(jnp.float32)
    enc_middle, enc_attn_store = self_forward(encoder_start, (gains[0], *whole[0:2]), enc_allowed, enc_live)
    encoder_final, enc_mlp_store = mlp_forward(enc_middle, (gains[1], *whole[2:4]), enc_live)
    decoder_start = dec_input.astype(jnp.float32)
    dec_middle, dec_self_store = self_forward(decoder_start, (gains[2], *whole[4:6]), self_allowed, dec_live)
    dec_crossed, cross_store = cross_forward(
        dec_middle, encoder_final, (gains[3], gains[4], *whole[6:9]), cross_allowed, dec_live
    )
    decoder_final, dec_mlp_store = mlp_forward(dec_crossed, (gains[5], *whole[9:11]), dec_live)
    grad_crossed, dec_mlp_grads = mlp_backward(
        dec_crossed, (gains[5], *whole[9:11]), dec_live, dec_mlp_store, dec_cotangent.astype(jnp.float32)
    )
    grad_middle, grad_memory, cross_grads = cross_backward(
        dec_middle,
        encoder_final,
        (gains[3], gains[4], *whole[6:9]),
        cross_allowed,
        dec_live,
        cross_store,
        grad_crossed,
    )
    grad_decoder_start, dec_self_grads = self_backward(
        decoder_start, (gains[2], *whole[4:6]), self_allowed, dec_live, dec_self_store, grad_middle
    )
    grad_enc_middle, enc_mlp_grads = mlp_backward(
        enc_middle,
        (gains[1], *whole[2:4]),
        enc_live,
        enc_mlp_store,
        enc_cotangent.astype(jnp.float32) + grad_memory,
    )
    grad_encoder_start, enc_attn_grads = self_backward(
        encoder_start, (gains[0], *whole[0:2]), enc_allowed, enc_live, enc_attn_store, grad_enc_middle
    )
    sums = enc_attn_grads + enc_mlp_grads + dec_self_grads + cross_grads + dec_mlp_grads
    summed = (scatter_all if linked else plain_scatter)(sums)
    grads, scale_grads = [], {}
    for total, shard, k in zip(summed, shards, SCALE_OF):
        if k is not None:
            scale_grads[k] = jnp.sum(total * shard.astype(jnp.float32), axis=1) / scales[k]
        grads.append(total)
    return (
        encoder_final.astype(jnp.bfloat16),
        decoder_final.astype(jnp.bfloat16),
        grad_encoder_start,
        grad_decoder_start,
        scale_grads[0], grads[0], grads[1],
        scale_grads[1], grads[2], grads[3],
        scale_grads[2], grads[4], grads[5],
        scale_grads[3], scale_grads[4], grads[6], grads[7], grads[8],
        scale_grads[5], grads[9], grads[10],
    )


def solution(mesh):
    rows, line = P(AXES, None), P(AXES)
    linked = mesh.shape["wide"] == 2 * Z and mesh.shape["narrow"] == 4
    weights = (
        line, rows, rows, line, rows, rows, line, rows, rows,
        line, line, rows, rows, rows, line, rows, rows,
    )
    return jax.shard_map(
        functools.partial(per_device, linked),
        mesh=mesh,
        in_specs=(rows, rows, line, line, *weights, rows, rows),
        out_specs=(rows, rows, rows, rows, *weights),
        check_vma=False,
    )
```

profile of v0, /device:TPU:0, one launch (start us, length us, event | category | flops | bytes accessed | tf_op | source)
XLA Modules:
  0.0 552.3 jit_solution(14549478205064533895)
XLA Ops:
  0.7 1.1 fusion.99
  1.8 1.2 fusion.81
  3.5 1.3 fusion.159
  6.8 1.2 compare_convert_fusion.3
  8.0 1.3 fusion.158
  18.2 179.6 %shard_map.382 = (bf16[4,2,2,2,3,8,2304]{6,5,4,3,2,1,0:T(8,128)(2,1)}, bf16[4,2,2,2,3,8,768]{6,5,4,3,2,1,0:T(8,128)(2,1)}, bf16[4,2,2,2,3,8,4096]{6,5,4,3,2,1,0:...) custom-call(bf16[3,8,2304]{2,1,0:T(8,128)(2,1)} %bitcast.248, ...), custom_call_target="tpu_custom_call" | custom-call | tf_op jit(solution)/shard_map/pallas_call | solution.py:393
  197.8 1.1 convert_reduce_fusion
  199.0 2.7 convolution_convert_fusion.5
  206.7 3.1 convolution_convert_fusion.4
  209.9 0.9 copy.78
  212.6 1.8 fusion.160
  218.3 1.9 fusion.153
  221.0 1.4 copy-done
  222.4 1.3 copy-done.135
  223.6 1.1 multiply_reduce_fusion.5
  227.5 1.9 copy.86
  230.3 1.7 fusion.162
  235.7 1.0 fusion.152
  237.6 1.6 fusion.110
  239.2 1.5 fusion.65
  240.7 2.3 multiply_reduce_fusion.10
  244.0 1.2 convolution_convert_fusion.20
  245.2 1.7 copy.87
  247.0 2.7 convolution_convert_fusion.15
  249.7 1.6 fusion.163
  251.3 12.1 %fusion.62 = bf16[12,64,128]{2,1,0:T(8,128)(2,1)} fusion(bf16[256,12,64]{0,2,1:T(8,128)(2,1)} %bitcast.216, f32[12,128,256]{2,1,0:T(8,128)} %fusion.163, f32[12,128,256]{2,1,0:T(8,128)} %copy-done.2, f32[12,128]{1,0:T(8,128)} %log_add_fusion.2), kind=kOutput, calls=%fused_computation.96 | convolution fusion | flops 53184256 | bytes 3741696 | tf_op jit(solution)/shard_map/hqk,khd->qhd/dot_general | solution.py:537
  263.4 12.1 %fusion.46 = bf16[12,64,256]{2,1,0:T(8,128)(2,1)} fusion(bf16[128,12,64]{0,2,1:T(8,128)(2,1)} %bitcast.238, f32[12,128,256]{2,1,0:T(8,128)} %fusion.163, f32[12,128,256]{2,1,0:T(8,128)} %copy-done.2, f32[12,128]{1,0:T(8,128)} %log_add_fusion.2), kind=kOutput, calls=%fused_computation.76 | convolution fusion | flops 53282560 | bytes 3741696 | tf_op jit(solution)/shard_map/hqk,qhd->khd/dot_general | solution.py:540
  275.5 4.5 multiply_reduce_fusion.4
  281.9 1.2 convolution_convert_fusion.19
  283.1 1.7 copy.92
  285.6 2.4 convolution_convert_fusion.16
  287.9 2.9 fusion.78
  290.9 4.1 fusion.92
  295.0 1.9 multiply_reduce_fusion.3
  298.6 1.3 convolution_convert_fusion.14
  299.9 1.9 copy.88
  301.8 2.3 fusion.165
  304.1 3.1 convolution_convert_fusion.18
  307.2 3.1 convolution_convert_fusion.17
  310.3 3.7 fusion.102
  315.0 1.4 fusion.50
  316.4 1.6 convolution_convert_fusion.11
  318.0 1.5 convolution_convert_fusion.12
  319.6 1.6 convolution_convert_fusion.10
  321.2 2.4 convolution_convert_fusion.6
  323.6 1.6 convolution_convert_fusion.13
  325.3 4.5 convolution_convert_fusion.1
  329.8 2.8 convolution_convert_fusion.7
  332.6 2.3 fusion.164
  334.9 5.2 fusion.53
  340.2 5.1 fusion.56
  345.3 3.7 fusion.84
  349.1 1.1 fusion.80
  350.3 3.0 convolution_convert_fusion.3
  353.4 2.8 convolution_convert_fusion.8
  356.2 2.9 convolution_convert_fusion.2
  359.2 4.6 convolution_convert_fusion
  363.8 170.8 %shard_map.383 = (f32[3,8,2304]{2,1,0:T(8,128)}, f32[3,8,768]{2,1,0:T(8,128)}, f32[3,8,4096]{2,1,0:T(8,128)}, f32[8,8,768]{2,1,0:T(8,128)}, f32[3,8,2304]{2,1,0:...) custom-call(bf16[4,2,2,2,3,8,2304]{6,5,4,3,2,1,0:T(8,128)(2,1)} %bit, ...), custom_call_target="tpu_custom_call" | custom-call | tf_op jit(solution)/shard_map/pallas_call | solution.py:452
  534.7 1.2 multiply_reduce_fusion.14
  536.4 1.2 multiply_reduce_fusion.8
  538.2 1.1 multiply_reduce_fusion.13
  539.8 1.0 multiply_reduce_fusion.16
  541.3 1.0 multiply_reduce_fusion.15
  542.9 1.2 multiply_reduce_fusion.7
  (373 shorter events, 45.1 us)
Async XLA Ops:
  0.7 198.3 %copy-start.20 = (bf16[128,768]{1,0:T(8,128)(2,1)S(1)}, bf16[128,768]{1,0:T(8,128)(2,1)}, u32[]{:S(2)}) copy-start(bf16[128,768]{1,0:T(8,128)(2,1)} %param.24) | copy-start | bytes 589828
  1.8 9.6 %copy-start.125 = (f32[128]{0:T(128)}, f32[128]{0:T(128)S(1)}, u32[]{:S(2)}) copy-start(f32[128]{0:T(128)S(1)} %fusion.99) | copy-start | bytes 1540
  1.8 199.9 %copy-start.112 = (f32[128]{0:T(128)}, f32[128]{0:T(128)S(1)}, u32[]{:S(2)}) copy-start(f32[128]{0:T(128)S(1)} %fusion.136) | copy-start | bytes 1540
  3.5 203.1 %copy-start.118 = (f32[256]{0:T(256)}, f32[256]{0:T(256)S(1)}, u32[]{:S(2)}) copy-start(f32[256]{0:T(256)S(1)} %fusion.132) | copy-start | bytes 3076
  11.3 192.4 %copy-start.97 = (f32[128]{0:T(128)}, f32[128]{0:T(128)S(1)}, u32[]{:S(2)}) copy-start(f32[128]{0:T(128)S(1)} %get-tuple-element.73) | copy-start | bytes 1540
  198.9 5.7 %copy-start.91 = (f32[768]{0:T(1024)}, f32[768]{0:T(1024)S(1)}, u32[]{:S(2)}) copy-start(f32[768]{0:T(1024)S(1)} %get-tuple-element.68) | copy-start | bytes 9220
  199.0 7.7 %copy-start.123 = (f32[768]{0:T(1024)}, f32[768]{0:T(1024)S(1)}, u32[]{:S(2)}) copy-start(f32[768]{0:T(1024)S(1)} %get-tuple-element.72) | copy-start | bytes 9220
  214.4 3.8 slice-start.2
  217.7 3.3 copy-start.10
  220.2 3.4 copy-start.135
  230.3 3.2 copy-start.52
  230.3 5.1 slice-start
  235.7 7.3 %copy-start.108 = (f32[128]{0:T(128)}, f32[128]{0:T(128)S(1)}, u32[]{:S(2)}) copy-start(f32[128]{0:T(128)S(1)} %fusion.138) | copy-start | bytes 1540
  275.4 4.6 copy-start.5
  275.4 4.6 copy-start.31
  275.4 4.6 copy-start.68
  275.4 4.6 copy-start.92
  285.6 5.3 copy-start.1
  285.6 5.3 copy-start.106
  287.9 7.0 %slice-start.4 = ((s8[6291456]{0:T(1024)(128)(4,1)}), s8[4194304]{0:T(1024)(128)(4,1)S(1)}, s32[]{:S(2)}) async-start(s8[6291456]{0:T(1024)(128)(4,1)} %bitcast.184), calls=%async_computation.4 | async-start | bytes 8388608
  290.8 6.3 %copy-start.18 = (f32[256,768]{1,0:T(8,128)}, f32[256,768]{1,0:T(8,128)S(1)}, u32[]{:S(2)}) copy-start(f32[256,768]{1,0:T(8,128)S(1)} %get-tuple-element.83) | copy-start | bytes 2359300
  290.8 4.2 slice-start.5
  290.8 4.2 copy-start.11
  310.2 3.8 copy-start.126
  310.2 3.8 copy-start.21
  310.2 3.8 copy-start.27
  310.2 3.8 copy-start.113
  310.3 4.7 copy-start.37
  310.3 4.7 copy-start.94
  316.4 3.2 copy-start.25
  316.4 3.2 copy-start.73
  318.0 3.2 copy-start.96
  321.2 4.1 copy-start.43
  321.2 4.0 copy-start.45
  325.2 4.6 copy-start.14
  325.3 4.6 copy-start.19
  340.2 5.1 copy-start.124
  345.2 3.8 copy-start.111
  345.2 3.8 copy-start.9
  345.2 3.8 copy-start.48
  345.2 3.8 copy-start.119
  363.7 171.0 %copy-start.75 = (bf16[24,2304]{1,0:T(8,128)(2,1)S(1)}, bf16[24,2304]{1,0:T(8,128)(2,1)}, u32[]{:S(2)}) copy-start(bf16[24,2304]{1,0:T(8,128)(2,1)} %param.28) | copy-start | bytes 331780
  363.7 172.1 %copy-start.129 = (bf16[24]{0:T(256)(128)(2,1)S(1)}, bf16[24]{0:T(256)(128)(2,1)}, u32[]{:S(2)}) copy-start(bf16[24]{0:T(256)(128)(2,1)} %param.27) | copy-start | bytes 148
  363.7 172.7 %copy-start.70 = (bf16[24,4096]{1,0:T(8,128)(2,1)S(1)}, bf16[24,4096]{1,0:T(8,128)(2,1)}, u32[]{:S(2)}) copy-start(bf16[24,4096]{1,0:T(8,128)(2,1)} %param.31) | copy-start | bytes 589828
  363.7 173.9 %copy-start.130 = (bf16[24]{0:T(256)(128)(2,1)S(1)}, bf16[24]{0:T(256)(128)(2,1)}, u32[]{:S(2)}) copy-start(bf16[24]{0:T(256)(128)(2,1)} %param.30) | copy-start | bytes 148
  363.8 174.4 %copy-start.76 = (bf16[24,2304]{1,0:T(8,128)(2,1)S(1)}, bf16[24,2304]{1,0:T(8,128)(2,1)}, u32[]{:S(2)}) copy-start(bf16[24,2304]{1,0:T(8,128)(2,1)} %param.34) | copy-start | bytes 331780
  363.8 175.5 %copy-start.131 = (bf16[24]{0:T(256)(128)(2,1)S(1)}, bf16[24]{0:T(256)(128)(2,1)}, u32[]{:S(2)}) copy-start(bf16[24]{0:T(256)(128)(2,1)} %param.33) | copy-start | bytes 148
  363.8 176.0 %copy-start.87 = (bf16[24,768]{1,0:T(8,128)(2,1)S(1)}, bf16[24,768]{1,0:T(8,128)(2,1)}, u32[]{:S(2)}) copy-start(bf16[24,768]{1,0:T(8,128)(2,1)} %param.38) | copy-start | bytes 110596
  363.8 177.0 %copy-start.132 = (bf16[24]{0:T(256)(128)(2,1)S(1)}, bf16[24]{0:T(256)(128)(2,1)}, u32[]{:S(2)}) copy-start(bf16[24]{0:T(256)(128)(2,1)} %param.36) | copy-start | bytes 148
  363.8 177.5 %copy-start.81 = (bf16[24,1536]{1,0:T(8,128)(2,1)S(1)}, bf16[24,1536]{1,0:T(8,128)(2,1)}, u32[]{:S(2)}) copy-start(bf16[24,1536]{1,0:T(8,128)(2,1)} %param.39) | copy-start | bytes 221188
  363.8 178.6 %copy-start.133 = (bf16[24]{0:T(256)(128)(2,1)S(1)}, bf16[24]{0:T(256)(128)(2,1)}, u32[]{:S(2)}) copy-start(bf16[24]{0:T(256)(128)(2,1)} %param.37) | copy-start | bytes 148
  363.8 179.1 %copy-start.71 = (bf16[24,4096]{1,0:T(8,128)(2,1)S(1)}, bf16[24,4096]{1,0:T(8,128)(2,1)}, u32[]{:S(2)}) copy-start(bf16[24,4096]{1,0:T(8,128)(2,1)} %param.42) | copy-start | bytes 589828
  534.7 9.4 %copy-start.134 = (bf16[24]{0:T(256)(128)(2,1)S(1)}, bf16[24]{0:T(256)(128)(2,1)}, u32[]{:S(2)}) copy-start(bf16[24]{0:T(256)(128)(2,1)} %param.41) | copy-start | bytes 148
  534.7 10.0 %copy-start.59 = (f32[3,8,2304]{2,1,0:T(8,128)S(1)}, f32[3,8,2304]{2,1,0:T(8,128)}, u32[]{:S(2)}) copy-start(f32[3,8,2304]{2,1,0:T(8,128)} %get-tuple-element.56) | copy-start | bytes 663556
  534.7 10.6 %copy-start.90 = (f32[3,8,768]{2,1,0:T(8,128)S(1)}, f32[3,8,768]{2,1,0:T(8,128)}, u32[]{:S(2)}) copy-start(f32[3,8,768]{2,1,0:T(8,128)} %get-tuple-element.57) | copy-start | bytes 221188
  534.7 11.3 %copy-start.50 = (f32[3,8,4096]{2,1,0:T(8,128)S(1)}, f32[3,8,4096]{2,1,0:T(8,128)}, u32[]{:S(2)}) copy-start(f32[3,8,4096]{2,1,0:T(8,128)} %get-tuple-element.58) | copy-start | bytes 1179652
  534.7 12.0 %copy-start.86 = (f32[8,8,768]{2,1,0:T(8,128)S(1)}, f32[8,8,768]{2,1,0:T(8,128)}, u32[]{:S(2)}) copy-start(f32[8,8,768]{2,1,0:T(8,128)} %get-tuple-element.59) | copy-start | bytes 589828
  534.7 12.7 %copy-start.58 = (f32[3,8,2304]{2,1,0:T(8,128)S(1)}, f32[3,8,2304]{2,1,0:T(8,128)}, u32[]{:S(2)}) copy-start(f32[3,8,2304]{2,1,0:T(8,128)} %get-tuple-element.60) | copy-start | bytes 663556
  535.9 12.2 %copy-start.89 = (f32[3,8,768]{2,1,0:T(8,128)S(1)}, f32[3,8,768]{2,1,0:T(8,128)}, u32[]{:S(2)}) copy-start(f32[3,8,768]{2,1,0:T(8,128)} %get-tuple-element.61) | copy-start | bytes 221188
  536.4 12.3 %copy-start.82 = (f32[3,8,768]{2,1,0:T(8,128)S(1)}, f32[3,8,768]{2,1,0:T(8,128)}, u32[]{:S(2)}) copy-start(f32[3,8,768]{2,1,0:T(8,128)} %get-tuple-element.62) | copy-start | bytes 221188
  536.4 12.9 %copy-start.74 = (f32[3,8,1536]{2,1,0:T(8,128)S(1)}, f32[3,8,1536]{2,1,0:T(8,128)}, u32[]{:S(2)}) copy-start(f32[3,8,1536]{2,1,0:T(8,128)} %get-tuple-element.63) | copy-start | bytes 442372
  537.6 12.4 %copy-start.88 = (f32[3,8,768]{2,1,0:T(8,128)S(1)}, f32[3,8,768]{2,1,0:T(8,128)}, u32[]{:S(2)}) copy-start(f32[3,8,768]{2,1,0:T(8,128)} %get-tuple-element.64) | copy-start | bytes 221188
  538.2 12.5 %copy-start.49 = (f32[3,8,4096]{2,1,0:T(8,128)S(1)}, f32[3,8,4096]{2,1,0:T(8,128)}, u32[]{:S(2)}) copy-start(f32[3,8,4096]{2,1,0:T(8,128)} %get-tuple-element.65) | copy-start | bytes 1179652
  542.9 8.5 %copy-start.85 = (f32[8,8,768]{2,1,0:T(8,128)S(1)}, f32[8,8,768]{2,1,0:T(8,128)}, u32[]{:S(2)}) copy-start(f32[8,8,768]{2,1,0:T(8,128)} %get-tuple-element.66) | copy-start | bytes 589828
  (80 other events, 153.1 us)
where the time goes:
time: 557 us; the launch traced here: 552 us
  Pallas kernels  350 us (63%)
  matrix products  128 us (23%)
  local copies, waits for them, and re-layouts  40.9 us (7%)
  other arithmetic  27.5 us (5%)
    pallas_call x1, Pallas kernels, gather_all(): pl.pallas_call(functools.partial(gather_body, PIECES, count), out_shape=s...  180 us
    pallas_call x1, Pallas kernels, scatter_all(): pl.pallas_call(functools.partial(scatter_body, pieces, count, stages), ou...  171 us
    dot_general x11, matrix products, outer_rows(): jnp.einsum('rd,re->de', left, right, preferred_element_type=jnp.float32)  29.4 us
    dot_general x11, matrix products, back_rows(): jnp.einsum('re,de->rd', incoming, matrix, preferred_element_type=jnp.floa...  26.3 us
    dot_general x3, matrix products, attend_backward(): jnp.einsum('hqk,khd->qhd', grad_scores, key_heads, preferred_element_type...  20.4 us
    dot_general x3, matrix products, attend_backward(): jnp.einsum('hqk,qhd->khd', grad_scores, query_heads, preferred_element_ty...  20.2 us
    unnamed x299, local copies, waits for them, and re-layouts  19.9 us

commit v1 on v0

--- a/solution.py
+++ b/solution.py
@@ -10,18 +10,22 @@
 D = 768
 HEADS = 12
 HEAD_DIM = 64
+FF = 2048
 AXES = ("wide", "narrow")
 MESH = pl.DeviceIdType.MESH
 
 Z = 4
 PIECES = (
     (11, 0, 768, False),
-    (0, 0, 1152, False), (0, 1152, 1152, False), (1, 0, 768, True),
-    (2, 0, 2048, False), (2, 2048, 2048, True), (3, 0, 768, False),
+    (0, 0, 1152, False), (0, 1152, 1152, True), (1, 0, 768, False),
+    (2, 0, 1024, False), (2, 1024, 1024, True), (2, 2048, 1024, False), (2, 3072, 1024, False),
+    (3, 0, 384, True), (3, 384, 384, False),
     (4, 0, 1152, False), (4, 1152, 1152, True), (5, 0, 768, False), (6, 0, 768, False),
-    (7, 0, 1536, True), (8, 0, 768, False),
-    (9, 0, 2048, False), (9, 2048, 2048, True), (10, 0, 768, False),
+    (7, 0, 768, True), (7, 768, 768, False), (8, 0, 768, False),
+    (9, 0, 1024, True), (9, 1024, 1024, False), (9, 2048, 1024, False), (9, 3072, 1024, True),
+    (10, 0, 384, False), (10, 384, 384, False),
 )
+STRIDE = 2
 
 
 class Place:
@@ -371,38 +375,269 @@
                 self.along_z(step, "wait_send")
 
 
-def gather_body(pieces, count, *refs):
-    parts, wholes = refs[:count], refs[count : 2 * count]
-    send, recv, local = refs[2 * count :]
+epsilon = 1e-06
+masked_value = -1000000000.0
+SHRINK = HEAD_DIM**-0.5
+NT = (((1,), (1,)), ((), ()))
+TN = (((0,), (0,)), ((), ()))
+f32, bf16 = jnp.float32, jnp.bfloat16
+
+
+def dot(a, b, dims=(((1,), (0,)), ((), ()))):
+    return lax.dot_general(a, b, dims, preferred_element_type=f32)
+
+
+def shrunk(values):
+    return lax.rsqrt(jnp.mean(values * values, axis=-1, keepdims=True) + epsilon)
+
+
+def norm(values, scales):
+    return values * shrunk(values) * scales
+
+
+def items_of(lengths_ref, places):
+    item, boundary = jnp.zeros_like(places), 0
+    for k in range(lengths_ref.shape[0]):
+        boundary = boundary + lengths_ref[k]
+        item = item + jnp.where(places >= boundary, 1, 0)
+    return item
+
+
+def fill_masks(enc_lengths, dec_lengths, enc_mask, self_mask, cross_mask):
+    count = enc_lengths.shape[0]
+
+    def grid(ref, axis):
+        return lax.broadcasted_iota(jnp.int32, ref.shape, axis)
+
+    def put(ref, rows, columns, both):
+        kept = rows == columns
+        if both is not None:
+            kept = kept & both
+        ref[...] = jnp.where(kept | (rows == count), 1.0, 0.0)
+
+    put(enc_mask, items_of(enc_lengths, grid(enc_mask, 0)), items_of(enc_lengths, grid(enc_mask, 1)), None)
+    put(
+        self_mask, items_of(dec_lengths, grid(self_mask, 0)), items_of(dec_lengths, grid(self_mask, 1)),
+        grid(self_mask, 1) <= grid(self_mask, 0),
+    )
+    put(cross_mask, items_of(dec_lengths, grid(cross_mask, 0)), items_of(enc_lengths, grid(cross_mask, 1)), None)
+
+
+def live_rows(lengths_ref, rows):
+    item = items_of(lengths_ref, lax.broadcasted_iota(jnp.int32, (rows, 1), 0))
+    return jnp.where(item < lengths_ref.shape[0], 1.0, 0.0)
+
+
+def head_lanes(which):
+    lanes = lax.broadcasted_iota(jnp.int32, (1, 2 * HEAD_DIM), 1)
+    return jnp.where(lanes // HEAD_DIM == which, 1.0, 0.0).astype(bf16)
+
+
+def head_probs(q, k, kept):
+    scores = jnp.where(kept[...] > 0.0, dot(q, k, NT) * SHRINK, masked_value)
+    raised = jnp.exp(scores - jnp.max(scores, axis=1, keepdims=True))
+    return raised * (1.0 / jnp.sum(raised, axis=1, keepdims=True))
+
+
+def pair_columns(pair, offset):
+    return pl.ds(pl.multiple_of(pair * (2 * HEAD_DIM) + offset, 2 * HEAD_DIM), 2 * HEAD_DIM)
+
+
+def attend(q_ref, q_at, k_ref, k_at, v_ref, v_at, kept, out_ref):
+    @pl.loop(0, HEADS // 2)
+    def _(pair):
+        q = q_ref[:, pair_columns(pair, q_at)]
+        k = k_ref[:, pair_columns(pair, k_at)]
+        v = v_ref[:, pair_columns(pair, v_at)]
+        mixed = None
+        for which in range(2):
+            lanes = head_lanes(which)
+            part = dot(head_probs(q * lanes, k, kept).astype(bf16), v * lanes)
+            mixed = part if mixed is None else mixed + part
+        out_ref[:, pair_columns(pair, 0)] = mixed.astype(bf16)
+
+
+def gelu_tanh(t):
+    return jnp.tanh(0.7978845608028654 * (t + 0.044715 * (t * t * t)))
+
+
+STORED = (
+    ("e_h1", "enc", D, bf16), ("e_qkv", "enc", 3 * D, bf16), ("e_o", "enc", D, bf16), ("e_x1", "enc", D, f32),
+    ("e_h2", "enc", D, bf16), ("e_u", "enc", 2 * FF, bf16), ("e_a", "enc", FF, bf16), ("e_x2", "enc", D, f32),
+    ("hm", "enc", D, bf16), ("kv", "enc", 2 * D, bf16),
+    ("d_h1", "dec", D, bf16), ("d_qkv", "dec", 3 * D, bf16), ("d_o", "dec", D, bf16), ("d_x1", "dec", D, f32),
+    ("hq", "dec", D, bf16), ("q", "dec", D, bf16), ("c_o", "dec", D, bf16), ("d_x2", "dec", D, f32),
+    ("d_h2", "dec", D, bf16), ("d_u", "dec", 2 * FF, bf16), ("d_a", "dec", FF, bf16),
+)
+
+
+class Forward:
+    def __init__(self, refs, lengths):
+        self.__dict__.update(refs)
+        self.lengths = lengths
+
+    def gain(self, k):
+        return self.gains[k : k + 1]
+
+    def set_norm(self, values, k, out):
+        out[...] = norm(values, self.gain(k)).astype(bf16)
+
+    def step(self, m, start, size, weight):
+        columns = pl.ds(start, size)
+        if m == 0 or m == 4:
+            side = "e" if m == 0 else "d"
+            if start == 0:
+                self.set_norm(getattr(self, side + "_x0")[...].astype(f32), 0 if m == 0 else 2, getattr(self, side + "_h1"))
+            qkv = getattr(self, side + "_qkv")
+            qkv[:, columns] = dot(getattr(self, side + "_h1")[...], weight).astype(bf16)
+            if start + size == qkv.shape[1]:
+                kept = self.enc_mask if m == 0 else self.self_mask
+                attend(qkv, 0, qkv, D, qkv, 2 * D, kept, getattr(self, side + "_o"))
+        elif m == 1:
+            self.e_x1[...] = self.e_x0[...].astype(f32) + self.live("enc") * dot(self.e_o[...], weight)
+            self.set_norm(self.e_x1[...], 1, self.e_h2)
+        elif m == 5:
+            self.d_x1[...] = self.d_x0[...].astype(f32) + self.live("dec") * dot(self.d_o[...], weight)
+            self.set_norm(self.d_x1[...], 3, self.hq)
+        elif m == 6:
+            self.q[...] = dot(self.hq[...], weight).astype(bf16)
+        elif m == 7:
+            self.kv[:, columns] = dot(self.hm[...], weight).astype(bf16)
+            if start + size == self.kv.shape[1]:
+                attend(self.q, 0, self.kv, 0, self.kv, D, self.cross_mask, self.c_o)
+        elif m == 8:
+            self.d_x2[...] = self.d_x1[...] + self.live("dec") * dot(self.c_o[...], weight)
+            self.set_norm(self.d_x2[...], 5, self.d_h2)
+        elif m == 2 or m == 9:
+            side = "e" if m == 2 else "d"
+            rows = getattr(self, side + "_h2").shape[0]
+            united = dot(getattr(self, side + "_h2")[...], weight)
+            getattr(self, side + "_u")[:, columns] = united.astype(bf16)
+            half = FF
+            if start < half:
+                self.gates[pl.ds(0, rows), columns] = united
+            else:
+                back = pl.ds(start - half, size)
+                gate = self.gates[pl.ds(0, rows), back]
+                getattr(self, side + "_a")[:, back] = (0.5 * gate * (1.0 + gelu_tanh(gate)) * united).astype(bf16)
+        else:
+            side, other = ("e", "enc") if m == 3 else ("d", "dec")
+            before = self.e_x1 if m == 3 else self.d_x2
+            after = before[:, columns] + self.live(other) * dot(getattr(self, side + "_a")[...], weight)
+            out = self.enc_out if m == 3 else self.dec_out
+            out[:, columns] = after.astype(bf16)
+            if m == 3:
+                self.e_x2[:, columns] = after
+                if start + size == D:
+                    self.set_norm(self.e_x2[...], 4, self.hm)
+
+    def live(self, side):
+        ref = self.e_x0 if side == "enc" else self.d_x0
+        return live_rows(self.lengths[side], ref.shape[0])
+
+
+def forward_body(pieces, count, *refs):
+    refs = list(refs)
+
+    def take(n):
+        got = refs[:n]
+        del refs[:n]
+        return got
+
+    parts = take(count)
+    e_x0, d_x0, enc_lengths, dec_lengths = take(4)
+    wholes = take(count)
+    stored = dict(zip([name for name, *_ in STORED], take(len(STORED))))
+    enc_out, dec_out, gains = take(3)
+    send, recv, local, stage_sem, spread, gates, enc_mask, self_mask, cross_mask, wide_stage, deep_stage = refs
     place = Place()
     place.barrier()
     work = [
         Gather(place, parts[m], wholes[m], pl.ds(start, size), z_first, (send, recv), k * Gather.SEMS, local.at[k])
         for k, (m, start, size, z_first) in enumerate(pieces)
     ]
-    for slot in range(len(work) + Gather.PHASES - 1):
-        for k in range(max(0, slot - Gather.PHASES + 1), min(slot, len(work) - 1) + 1):
-            work[k].phase(slot - k)
-
-
-def gather_all(shards):
+    forward = Forward(
+        dict(
+            stored, e_x0=e_x0, d_x0=d_x0, enc_out=enc_out, dec_out=dec_out, gains=gains, gates=gates,
+            enc_mask=enc_mask, self_mask=self_mask, cross_mask=cross_mask,
+        ),
+        {"enc": enc_lengths, "dec": dec_lengths},
+    )
+
+    def staged(k):
+        m, start, size, _ = pieces[k]
+        if m == len(parts) - 1:
+            into = spread
+        elif parts[m].shape[0] > 3:
+            into = deep_stage.at[k % STAGES, ..., pl.ds(0, size)]
+        else:
+            into = wide_stage.at[k % STAGES, ..., pl.ds(0, size)]
+        return pltpu.make_async_copy(wholes[m].at[..., pl.ds(start, size)], into, stage_sem.at[k % STAGES])
+
+    last = STRIDE * (Gather.PHASES - 1)
+    for slot in range(len(work) + last + 1):
+        for k in range(len(work)):
+            if (slot - k) % STRIDE == 0 and 0 <= slot - k <= last:
+                work[k].phase((slot - k) // STRIDE)
+        if slot == 0:
+            fill_masks(enc_lengths, dec_lengths, enc_mask, self_mask, cross_mask)
+        if 0 <= slot - last < len(work):
+            staged(slot - last).start()
+        k = slot - last - 1
+        if k >= 0:
+            staged(k).wait()
+            m, start, size, _ = pieces[k]
+            if m == len(parts) - 1:
+                gains[...] = jnp.sum(spread[...].reshape(-1, 8, D).astype(f32), axis=0)
+            else:
+                stage = deep_stage if parts[m].shape[0] > 3 else wide_stage
+                weight = stage[k % STAGES, ..., pl.ds(0, size)]
+                forward.step(m, start, size, weight.reshape(-1, size))
+
+
+STAGES = 2
+
+
+def forward_all(shards, enc_input, dec_input, enc_lengths, dec_lengths):
     count = len(shards)
     parts = [s.reshape(s.shape[0] // 8, 8, s.shape[1]) for s in shards]
-    shapes = [jax.ShapeDtypeStruct((Z, 2, 2, 2, *p.shape), p.dtype) for p in parts]
     sems = len(PIECES) * Gather.SEMS
-    wholes = pl.pallas_call(
-        functools.partial(gather_body, PIECES, count),
-        out_shape=shapes,
-        in_specs=[pl.BlockSpec(memory_space=pl.ANY)] * count,
-        out_specs=[pl.BlockSpec(memory_space=pl.ANY)] * count,
+    rows = {"enc": enc_input.shape[0], "dec": dec_input.shape[0]}
+    hbm, vmem = pl.BlockSpec(memory_space=pl.ANY), pl.BlockSpec(memory_space=pltpu.VMEM)
+    smem = pl.BlockSpec(memory_space=pltpu.SMEM)
+    widest = max(size for m, _, size, _ in PIECES if parts[m].shape[0] == 3)
+    deep = max((parts[m].shape[0], size) for m, _, size, _ in PIECES)
+    outs = pl.pallas_call(
+        functools.partial(forward_body, PIECES, count),
+        out_shape=[jax.ShapeDtypeStruct((Z, 2, 2, 2, *p.shape), p.dtype) for p in parts]
+        + [jax.ShapeDtypeStruct((rows[side], columns), dtype) for _, side, columns, dtype in STORED]
+        + [
+            jax.ShapeDtypeStruct(enc_input.shape, bf16),
+            jax.ShapeDtypeStruct(dec_input.shape, bf16),
+            jax.ShapeDtypeStruct((8, D), f32),
+        ],
+        in_specs=[hbm] * count + [vmem, vmem, smem, smem],
+        out_specs=[hbm] * count + [vmem] * (len(STORED) + 3),
         scratch_shapes=[
             pltpu.SemaphoreType.DMA((sems,)),
             pltpu.SemaphoreType.DMA((sems,)),
             pltpu.SemaphoreType.DMA((len(PIECES),)),
+            pltpu.SemaphoreType.DMA((STAGES,)),
+            pltpu.VMEM((Z, 2, 2, 2, 1, 8, D), bf16),
+            pltpu.VMEM((rows["enc"], FF), f32),
+            pltpu.VMEM((rows["enc"], rows["enc"]), f32),
+            pltpu.VMEM((rows["dec"], rows["dec"]), f32),
+            pltpu.VMEM((rows["dec"], rows["enc"]), f32),
+            pltpu.VMEM((STAGES, Z, 2, 2, 2, 3, 8, widest), bf16),
+            pltpu.VMEM((STAGES, Z, 2, 2, 2, deep[0], 8, deep[1]), bf16),
         ],
-        compiler_params=pltpu.CompilerParams(collective_id=0, has_side_effects=True),
-    )(*parts)
-    return [w.reshape(-1, w.shape[-1]) for w in wholes]
+        compiler_params=pltpu.CompilerParams(
+            collective_id=0, has_side_effects=True, vmem_limit_bytes=60 * 2**20
+        ),
+    )(*parts, enc_input, dec_input, enc_lengths, dec_lengths)
+    wholes, stored, (enc_out, dec_out, gains) = outs[:count], outs[count:-3], outs[-3:]
+    stored = dict(zip([name for name, *_ in STORED], stored))
+    return wholes, stored, enc_out, dec_out, gains
 
 
 def scatter_body(pieces, count, stages, *refs):
@@ -416,16 +651,17 @@
     work = []
     for k, (m, start, size, z_first) in enumerate(pieces):
         total, lasts, zs, firsts = (scratch.pop(0) for _ in range(4))
-        mine = mines[(sums[m].shape[4], size)]
+        mine = mines[(sums[m].shape[4], size)].at[k % STRIDE]
         work.append(
             Scatter(
                 place, sums[m], pl.ds(start, size), z_first, outs[m], total, mine, lasts, zs, firsts,
                 (send, recv), k * Scatter.SEMS, local.at[k],
             )
         )
-    for slot in range(len(work) + Scatter.PHASES - 1):
-        for k in range(max(0, slot - Scatter.PHASES + 1), min(slot, len(work) - 1) + 1):
-            work[k].phase(slot - k)
+    for slot in range(len(work) + STRIDE * (Scatter.PHASES - 1)):
+        for k in range(len(work)):
+            if (slot - k) % STRIDE == 0 and 0 <= slot - k <= STRIDE * (Scatter.PHASES - 1):
+                work[k].phase((slot - k) // STRIDE)
 
 
 def scatter_all(sums):
@@ -440,7 +676,7 @@
         pltpu.SemaphoreType.DMA((sems,)),
         pltpu.SemaphoreType.DMA((len(pieces),)),
     ]
-    scratch += [pltpu.VMEM((Z, 2, 2, r, 8, size), jnp.bfloat16) for r, size in stages]
+    scratch += [pltpu.VMEM((STRIDE, Z, 2, 2, r, 8, size), jnp.bfloat16) for r, size in stages]
     for m, _, size, z_first in pieces:
         block = (groups[m], 8, size)
         scratch += [
@@ -460,10 +696,6 @@
         ),
     )(*parts)
     return [o.reshape(-1, o.shape[-1]) for o in outs]
-
-
-epsilon = 1e-06
-masked_value = -1000000000.0
 
 
 def norm_rows(values, scales):
@@ -703,20 +935,40 @@
         columns = jnp.arange(D, dtype=jnp.int32) // scales[0].shape[0] == mine
         rows = [jnp.where(columns, jnp.tile(g, D // g.shape[0]), 0.0) for g in scales]
         rows += [jnp.zeros((D,), jnp.float32)] * (8 - len(rows))
-        *whole, spread = gather_all((*shards, jnp.stack(rows).astype(jnp.bfloat16)))
-        gains = jnp.sum(spread.reshape(-1, 8, D).astype(jnp.float32), axis=0)
+        packed = jnp.stack(rows).astype(jnp.bfloat16)
+        (*whole, _), kept, enc_out, dec_out, gains = forward_all(
+            (*shards, packed), enc_input, dec_input, enc_lengths, dec_lengths
+        )
+        whole = [w.reshape(-1, w.shape[-1]) for w in whole]
     else:
         whole = plain_gather(shards)
         gains = plain_gather(scales)
     encoder_start = enc_input.astype(jnp.float32)
-    enc_middle, enc_attn_store = self_forward(encoder_start, (gains[0], *whole[0:2]), enc_allowed, enc_live)
-    encoder_final, enc_mlp_store = mlp_forward(enc_middle, (gains[1], *whole[2:4]), enc_live)
     decoder_start = dec_input.astype(jnp.float32)
-    dec_middle, dec_self_store = self_forward(decoder_start, (gains[2], *whole[4:6]), self_allowed, dec_live)
-    dec_crossed, cross_store = cross_forward(
-        dec_middle, encoder_final, (gains[3], gains[4], *whole[6:9]), cross_allowed, dec_live
-    )
-    decoder_final, dec_mlp_store = mlp_forward(dec_crossed, (gains[5], *whole[9:11]), dec_live)
+    if linked:
+        g = kept
+        enc_middle, encoder_final, dec_middle, dec_crossed = g["e_x1"], g["e_x2"], g["d_x1"], g["d_x2"]
+
+        def logs(q, k, allowed):
+            scores = score_rows(head_split(q), head_split(k), allowed)
+            return jax.nn.logsumexp(scores, axis=2, keepdims=True)
+
+        enc_attn_store = (g["e_h1"], g["e_qkv"], g["e_o"], logs(g["e_qkv"][:, :D], g["e_qkv"][:, D:2*D], enc_allowed))
+        enc_mlp_store = (g["e_h2"], g["e_u"].astype(jnp.float32), g["e_a"])
+        dec_self_store = (g["d_h1"], g["d_qkv"], g["d_o"], logs(g["d_qkv"][:, :D], g["d_qkv"][:, D:2*D], self_allowed))
+        cross_store = (g["hq"], g["hm"], g["q"], g["kv"], g["c_o"], logs(g["q"], g["kv"][:, :D], cross_allowed))
+        dec_mlp_store = (g["d_h2"], g["d_u"].astype(jnp.float32), g["d_a"])
+    else:
+        encoder_start = enc_input.astype(jnp.float32)
+        enc_middle, enc_attn_store = self_forward(encoder_start, (gains[0], *whole[0:2]), enc_allowed, enc_live)
+        encoder_final, enc_mlp_store = mlp_forward(enc_middle, (gains[1], *whole[2:4]), enc_live)
+        decoder_start = dec_input.astype(jnp.float32)
+        dec_middle, dec_self_store = self_forward(decoder_start, (gains[2], *whole[4:6]), self_allowed, dec_live)
+        dec_crossed, cross_store = cross_forward(
+            dec_middle, encoder_final, (gains[3], gains[4], *whole[6:9]), cross_allowed, dec_live
+        )
+        decoder_final, dec_mlp_store = mlp_forward(dec_crossed, (gains[5], *whole[9:11]), dec_live)
+        enc_out, dec_out = encoder_final.astype(jnp.bfloat16), decoder_final.astype(jnp.bfloat16)
     grad_crossed, dec_mlp_grads = mlp_backward(
         dec_crossed, (gains[5], *whole[9:11]), dec_live, dec_mlp_store, dec_cotangent.astype(jnp.float32)
     )
@@ -750,8 +1002,8 @@
             scale_grads[k] = jnp.sum(total * shard.astype(jnp.float32), axis=1) / scales[k]
         grads.append(total)
     return (
-        encoder_final.astype(jnp.bfloat16),
-        decoder_final.astype(jnp.bfloat16),
+        enc_out,
+        dec_out,
         grad_encoder_start,
         grad_decoder_start,
         scale_grads[0], grads[0], grads[1],

time: 557 us -> 448 us (0.80)
  Pallas kernels: 350 us -> 298 us
  matrix products: 128 us -> 93.8 us
  local copies, waits for them, and re-layouts: 40.9 us -> 22.8 us
  other arithmetic: 27.5 us -> 19.5 us
    pallas_call x1, Pallas kernels: 171 us -> 140 us  [scatter_all(): pl.pallas_call(functools.partial(scatter_body, pieces, count, stages), ou...]
    pallas_call x1, Pallas kernels: 180 us -> 158 us  [forward_all(): pl.pallas_call(functools.partial(forward_body, PIECES, count), out_shape=...]
    dot_general x14 -> x0, matrix products: 15.7 us -> none  [the longest x2 5.81 us: self_forward(): jnp.dot(normed, joined, preferred_element_type=jnp.float32)]
    unnamed x299 -> x207, local copies, waits for them, and re-layouts: 19.9 us -> 12 us
    dot_general x11, matrix products: 26.3 us -> 18.7 us  [back_rows(): jnp.einsum('re,de->rd', incoming, matrix, preferred_element_type=jnp.floa...]
where the time goes in v1:
time: 448 us; the launch traced here: 439 us
  Pallas kernels  298 us (67%)
  matrix products  93.8 us (21%)
  local copies, waits for them, and re-layouts  22.8 us (5%)
  other arithmetic  19.5 us (4%)
  between operations  4.74 us (1%)
    pallas_call x1, Pallas kernels, forward_all(): pl.pallas_call(functools.partial(forward_body, PIECES, count), out_shape=...  158 us
    pallas_call x1, Pallas kernels, scatter_all(): pl.pallas_call(functools.partial(scatter_body, pieces, count, stages), ou...  140 us
    dot_general x11, matrix products, outer_rows(): jnp.einsum('rd,re->de', left, right, preferred_element_type=jnp.float32)  30.1 us
    dot_general x11, matrix products, back_rows(): jnp.einsum('re,de->rd', incoming, matrix, preferred_element_type=jnp.floa...  18.7 us
    dot_general x3, matrix products, attend_backward(): jnp.einsum('hqk,qhd->khd', grad_scores, query_heads, preferred_element_ty...  17.8 us
    dot_general x3, matrix products, attend_backward(): jnp.einsum('hqk,khd->qhd', grad_scores, key_heads, preferred_element_type...  17.1 us
    unnamed x207, local copies, waits for them, and re-layouts  12 us

profile of v1, /device:TPU:0, one launch (start us, length us, event | category | flops | bytes accessed | tf_op | source)
XLA Modules:
  0.0 438.7 jit_solution(7270650998349678623)
XLA Ops:
  0.7 0.7 tile.62
  1.4 0.7 tile.64
  2.2 0.7 tile.28
  3.0 0.7 tile.60
  3.8 0.7 tile.24
  4.5 0.7 tile.26
  5.3 0.6 stack.31.refs_11_
  6.0 157.6 %shard_map.382 = (bf16[4,2,2,2,3,8,2304]{6,5,4,3,2,1,0:T(8,128)(2,1)}, bf16[4,2,2,2,3,8,768]{6,5,4,3,2,1,0:T(8,128)(2,1)}, bf16[4,2,2,2,3,8,4096]{6,5,4,3,2,1,0:...) custom-call(bf16[3,8,2304]{2,1,0:T(8,128)(2,1)} %bitcast.203, ...), custom_call_target="tpu_custom_call" | custom-call | tf_op jit(solution)/shard_map/pallas_call | solution.py:610
  163.5 2.9 convert_element_type.252
  168.3 0.7 broadcast_compare_fusion.1
  169.1 4.1 multiply_multiply_fusion.5
  173.2 0.7 slice_reduce_fusion
  173.9 2.3 multiply_reduce_fusion.12
  177.7 1.6 fusion.143
  181.5 0.7 fusion.96
  183.4 11.1 %fusion.37 = bf16[12,64,256]{2,1,0:T(8,128)(2,1)} fusion(bf16[128,12,64]{0,2,1:T(8,128)(2,1)S(1)} %bitcast.189, f32[12,128,256]{2,1,0:T(8,128)} %fusion.143, f32[12,128,256]{2,1,0:T(8,128)S(1)} %get-tuple-element.163, f32[12,128]{1,0:T(8,128)S(1)} %log_add_fusion.2), kind=kOutput, calls=%fused_computation.58 | convolution fusion | flops 53282560 | bytes 3741696 | tf_op jit(solution)/shard_map/hqk,qhd->khd/dot_general | solution.py:772
  195.4 2.4 convolution_convert_fusion.4
  197.9 10.4 %fusion.49 = bf16[12,64,128]{2,1,0:T(8,128)(2,1)S(1)} fusion(bf16[256,12,64]{0,2,1:T(8,128)(2,1)S(1)} %bitcast.173, f32[12,128,256]{2,1,0:T(8,128)} %fusion.143, f32[12,128,256]{2,1,0:T(8,128)S(1)} %get-tuple-element.163, f32[12,128]{1,0:T(8,128)S(1)} %log_add_fusion.2), kind=kOutput, calls=%fused_computation.74 | convolution fusion | flops 53184256 | bytes 3741696 | tf_op jit(solution)/shard_map/hqk,khd->qhd/dot_general | solution.py:769
  208.3 1.5 convolution_convert_fusion.8
  209.8 0.6 multiply_reduce_fusion.10
  210.8 1.6 convolution_convert_fusion.9
  214.5 1.1 convolution_convert_fusion.15
  215.6 1.1 convolution_convert_fusion.14
  217.1 4.0 convolution_convert_fusion.2
  221.2 0.9 multiply_reduce_fusion.6
  222.4 0.7 compare_convert_fusion
  223.3 2.9 convolution_convert_fusion.5
  226.2 1.5 convolution_convert_fusion.7
  228.5 2.3 multiply_multiply_fusion.2
  230.9 4.5 %convolution_convert_fusion.1 = bf16[768,4096]{1,0:T(8,128)(2,1)} fusion(bf16[256,768]{1,0:T(8,128)(2,1)S(1)} %copy-done.44, f32[256,2048]{1,0:T(8,128)S(1)} %get-tuple-element.134, f32[256,2048]{1,0:T(8,128)S(1)} %get-tuple-element.133), kind=kOutput, calls=%fused_computation.4 | convolution fusion | flops 1615855616 | bytes 10878976 | tf_op jit(solution)/shard_map/rd,re->de/dot_general | solution.py:729
  235.4 2.0 multiply_reduce_fusion.4
  237.6 0.7 copy-done.43
  238.4 1.6 convolution_convert_fusion.10
  241.6 2.3 fusion.144
  243.9 0.9 copy.75
  244.8 0.9 copy.76
  245.8 1.8 fusion.6
  247.7 0.7 exponential_reduce_fusion
  248.4 5.7 %fusion.43 = bf16[12,64,256]{2,1,0:T(8,128)(2,1)} fusion(bf16[256,12,64]{0,2,1:T(8,128)(2,1)} %bitcast.178, f32[12,256,256]{1,2,0:T(8,128)} %fusion.144, f32[12,256,256]{1,2,0:T(8,128)S(1)} %get-tuple-element.167, f32[12,256]{1,0:T(8,128)S(1)} %log_add_fusion, pred[256,256]{0,1:T(8,128)(4,1)} %copy-done.31), kind=kOutput, calls=%fused_computation.60 | convolution fusion | flops 109513984 | bytes 7155712 | tf_op jit(solution)/shard_map/hqk,khd->qhd/dot_general | solution.py:769
  254.0 5.7 %fusion.46 = bf16[12,64,256]{2,1,0:T(8,128)(2,1)} fusion(bf16[256,12,64]{0,2,1:T(8,128)(2,1)} %bitcast.180, f32[12,256,256]{1,2,0:T(8,128)} %fusion.144, f32[12,256,256]{1,2,0:T(8,128)S(1)} %get-tuple-element.167, f32[12,256]{1,0:T(8,128)S(1)} %log_add_fusion, pred[256,256]{0,1:T(8,128)(4,1)} %copy-done.31), kind=kOutput, calls=%fused_computation.61 | convolution fusion | flops 109513984 | bytes 7155712 | tf_op jit(solution)/shard_map/hqk,qhd->khd/dot_general | solution.py:772
  259.7 2.3 fusion.40
  262.1 3.0 convolution_convert_fusion.3
  265.1 4.5 %convolution_convert_fusion = bf16[768,4096]{1,0:T(8,128)(2,1)} fusion(bf16[128,768]{1,0:T(8,128)(2,1)S(1)} %copy-done.45, f32[128,2048]{1,0:T(8,128)S(1)} %copy-done.5, f32[128,2048]{1,0:T(8,128)S(1)} %copy-done.3), kind=kOutput, calls=%fused_computation.3 | convolution fusion | flops 809500672 | bytes 8585216 | tf_op jit(solution)/shard_map/rd,re->de/dot_general | solution.py:729
  269.6 2.7 convolution_convert_fusion.6
  272.4 140.3 %shard_map.383 = (f32[3,8,2304]{2,1,0:T(8,128)}, f32[3,8,768]{2,1,0:T(8,128)}, f32[3,8,4096]{2,1,0:T(8,128)}, f32[8,8,768]{2,1,0:T(8,128)}, f32[3,8,2304]{2,1,0:...) custom-call(bf16[4,2,2,2,3,8,2304]{6,5,4,3,2,1,0:T(8,128)(2,1)} %bit, ...), custom_call_target="tpu_custom_call" | custom-call | tf_op jit(solution)/shard_map/pallas_call | solution.py:688
  412.8 1.2 multiply_reduce_fusion.7
  414.6 1.0 multiply_reduce_fusion.15
  416.1 1.0 multiply_reduce_fusion.16
  417.7 1.1 multiply_reduce_fusion.13
  419.3 1.1 multiply_reduce_fusion.8
  421.0 1.1 multiply_reduce_fusion.14
  422.6 3.6 fusion.80
  426.2 0.9 fusion.82
  427.2 1.2 fusion.66
  428.5 1.1 fusion.68
  429.6 0.7 copy.108
  430.4 0.7 copy.109
  431.1 0.7 copy.110
  432.4 0.7 copy.112
  433.2 0.7 copy.113
  433.8 0.7 copy.114
  435.8 0.7 copy.117
  437.1 0.7 copy.119
  437.8 0.7 copy.120
  (261 shorter events, 17.6 us)
Async XLA Ops:
  6.0 160.5 %copy-start.69 = (s32[2]{0:T(128)S(1)}, s32[2]{0:T(128)}, u32[]{:S(2)}) copy-start(s32[2]{0:T(128)} %refs_15_.1) | copy-start | bytes 28
  6.0 163.0 %copy-start.21 = (bf16[128,768]{1,0:T(8,128)(2,1)S(1)}, bf16[128,768]{1,0:T(8,128)(2,1)}, u32[]{:S(2)}) copy-start(bf16[128,768]{1,0:T(8,128)(2,1)} %param.45) | copy-start | bytes 589828
  163.5 10.4 %slice-start = ((s8[6291456]{0:T(1024)(128)(4,1)}), s8[2097152]{0:T(1024)(128)(4,1)S(1)}, s32[]{:S(2)}) async-start(s8[6291456]{0:T(1024)(128)(4,1)} %bitcast.156), calls=%async_computation | async-start | bytes 4194304
  169.0 13.2 %copy-start.67 = (s32[128]{0:T(128)}, s32[128]{0:T(128)S(1)}, u32[]{:S(2)}) copy-start(s32[128]{0:T(128)S(1)} %get-tuple-element.132) | copy-start | bytes 1540
  169.0 13.2 %copy-start.71 = (pred[128]{0:T(512)(128)(4,1)}, pred[128]{0:T(512)(128)(4,1)S(1)}, u32[]{:S(2)}) copy-start(pred[128]{0:T(512)(128)(4,1)S(1)} %get-tuple-element.131) | copy-start | bytes 388
  169.0 7.5 %copy-start.63 = (f32[128]{0:T(128)}, f32[128]{0:T(128)S(1)}, u32[]{:S(2)}) copy-start(f32[128]{0:T(128)S(1)} %compare_convert_fusion.1) | copy-start | bytes 1540
  169.0 4.1 copy-start.62
  169.0 4.9 %slice-start.1 = ((s8[6291456]{0:T(1024)(128)(4,1)}), s8[4194304]{0:T(1024)(128)(4,1)S(1)}, s32[]{:S(2)}) async-start(s8[6291456]{0:T(1024)(128)(4,1)} %bitcast.156), calls=%async_computation.1 | async-start | bytes 8388608
  169.1 4.9 %copy-start.8 = (f32[128,768]{1,0:T(8,128)S(1)}, f32[128,768]{1,0:T(8,128)}, u32[]{:S(2)}) copy-start(f32[128,768]{1,0:T(8,128)} %get-tuple-element.75) | copy-start | bytes 1179652
  173.2 3.1 copy-start.2
  173.2 3.1 copy-start.4
  183.3 11.6 %copy-start.39 = (bf16[256,768]{1,0:T(8,128)(2,1)S(1)}, bf16[256,768]{1,0:T(8,128)(2,1)}, u32[]{:S(2)}) copy-start(bf16[256,768]{1,0:T(8,128)(2,1)} %get-tuple-element.98) | copy-start | bytes 1179652
  197.9 10.4 %copy-start.48 = (bf16[128,768]{1,0:T(8,128)(2,1)S(1)}, bf16[128,768]{1,0:T(8,128)(2,1)}, u32[]{:S(2)}) copy-start(bf16[128,768]{1,0:T(8,128)(2,1)} %get-tuple-element.97) | copy-start | bytes 589828
  197.9 11.9 %copy-start.12 = (f32[128,768]{1,0:T(8,128)S(1)}, f32[128,768]{1,0:T(8,128)}, u32[]{:S(2)}) copy-start(f32[128,768]{1,0:T(8,128)} %get-tuple-element.87) | copy-start | bytes 1179652
  217.0 4.1 copy-start.29
  217.1 4.0 copy-start.25
  217.1 4.0 copy-start.41
  217.1 4.0 copy-start.76
  217.1 4.0 copy-start.85
  223.3 4.4 %copy-start.7 = (bf16[256,4096]{1,0:T(8,128)(2,1)S(1)}, bf16[256,4096]{1,0:T(8,128)(2,1)}, u32[]{:S(2)}) copy-start(bf16[256,4096]{1,0:T(8,128)(2,1)} %get-tuple-element.79) | copy-start | bytes 6291460
  227.7 7.6 %slice-start.2 = ((s8[6291456]{0:T(1024)(128)(4,1)}), s8[4194304]{0:T(1024)(128)(4,1)S(1)}, s32[]{:S(2)}) async-start(s8[6291456]{0:T(1024)(128)(4,1)} %bitcast.223), calls=%async_computation.2 | async-start | bytes 8388608
  228.5 6.8 %slice-start.3 = ((s8[6291456]{0:T(1024)(128)(4,1)}), s8[2097152]{0:T(1024)(128)(4,1)S(1)}, s32[]{:S(2)}) async-start(s8[6291456]{0:T(1024)(128)(4,1)} %bitcast.223), calls=%async_computation.3 | async-start | bytes 4194304
  230.9 4.5 %copy-start.24 = (f32[256,768]{1,0:T(8,128)S(1)}, f32[256,768]{1,0:T(8,128)}, u32[]{:S(2)}) copy-start(f32[256,768]{1,0:T(8,128)} %get-tuple-element.82) | copy-start | bytes 2359300
  230.9 4.5 %copy-start.75 = (f32[768]{0:T(1024)S(1)}, f32[768]{0:T(1024)}, u32[]{:S(2)}) copy-start(f32[768]{0:T(1024)} %get-tuple-element.128) | copy-start | bytes 9220
  240.7 3.1 copy-start.13
  262.0 3.1 copy-start.91
  262.1 3.0 copy-start.3
  262.1 3.0 copy-start.5
  265.1 4.5 %copy-start.22 = (bf16[128,768]{1,0:T(8,128)(2,1)S(1)}, bf16[128,768]{1,0:T(8,128)(2,1)}, u32[]{:S(2)}) copy-start(bf16[128,768]{1,0:T(8,128)(2,1)} %param.45) | copy-start | bytes 589828
  265.1 4.5 %copy-start.35 = (bf16[128,2048]{1,0:T(8,128)(2,1)S(1)}, bf16[128,2048]{1,0:T(8,128)(2,1)}, u32[]{:S(2)}) copy-start(bf16[128,2048]{1,0:T(8,128)(2,1)} %get-tuple-element.101) | copy-start | bytes 1572868
  265.1 4.5 %copy-start.66 = (f32[128]{0:T(128)S(1)}, f32[128]{0:T(128)}, u32[]{:S(2)}) copy-start(f32[128]{0:T(128)} %copy-done.63) | copy-start | bytes 1540
  272.3 140.5 %copy-start.27 = (bf16[24,4096]{1,0:T(8,128)(2,1)S(1)}, bf16[24,4096]{1,0:T(8,128)(2,1)}, u32[]{:S(2)}) copy-start(bf16[24,4096]{1,0:T(8,128)(2,1)} %param.42) | copy-start | bytes 589828
  272.3 141.8 %copy-start.77 = (bf16[24]{0:T(256)(128)(2,1)S(1)}, bf16[24]{0:T(256)(128)(2,1)}, u32[]{:S(2)}) copy-start(bf16[24]{0:T(256)(128)(2,1)} %param.41) | copy-start | bytes 148
  272.3 142.3 %copy-start.46 = (bf16[24,1536]{1,0:T(8,128)(2,1)S(1)}, bf16[24,1536]{1,0:T(8,128)(2,1)}, u32[]{:S(2)}) copy-start(bf16[24,1536]{1,0:T(8,128)(2,1)} %param.39) | copy-start | bytes 221188
  272.3 143.3 %copy-start.78 = (bf16[24]{0:T(256)(128)(2,1)S(1)}, bf16[24]{0:T(256)(128)(2,1)}, u32[]{:S(2)}) copy-start(bf16[24]{0:T(256)(128)(2,1)} %param.37) | copy-start | bytes 148
  272.3 143.9 %copy-start.58 = (bf16[24,768]{1,0:T(8,128)(2,1)S(1)}, bf16[24,768]{1,0:T(8,128)(2,1)}, u32[]{:S(2)}) copy-start(bf16[24,768]{1,0:T(8,128)(2,1)} %param.38) | copy-start | bytes 110596
  272.3 144.9 %copy-start.79 = (bf16[24]{0:T(256)(128)(2,1)S(1)}, bf16[24]{0:T(256)(128)(2,1)}, u32[]{:S(2)}) copy-start(bf16[24]{0:T(256)(128)(2,1)} %param.36) | copy-start | bytes 148
  272.3 145.4 %copy-start.36 = (bf16[24,2304]{1,0:T(8,128)(2,1)S(1)}, bf16[24,2304]{1,0:T(8,128)(2,1)}, u32[]{:S(2)}) copy-start(bf16[24,2304]{1,0:T(8,128)(2,1)} %param.34) | copy-start | bytes 331780
  272.3 146.4 %copy-start.80 = (bf16[24]{0:T(256)(128)(2,1)S(1)}, bf16[24]{0:T(256)(128)(2,1)}, u32[]{:S(2)}) copy-start(bf16[24]{0:T(256)(128)(2,1)} %param.33) | copy-start | bytes 148
  272.3 147.0 %copy-start.28 = (bf16[24,4096]{1,0:T(8,128)(2,1)S(1)}, bf16[24,4096]{1,0:T(8,128)(2,1)}, u32[]{:S(2)}) copy-start(bf16[24,4096]{1,0:T(8,128)(2,1)} %param.31) | copy-start | bytes 589828
  272.3 148.1 %copy-start.81 = (bf16[24]{0:T(256)(128)(2,1)S(1)}, bf16[24]{0:T(256)(128)(2,1)}, u32[]{:S(2)}) copy-start(bf16[24]{0:T(256)(128)(2,1)} %param.30) | copy-start | bytes 148
  272.3 148.6 %copy-start.37 = (bf16[24,2304]{1,0:T(8,128)(2,1)S(1)}, bf16[24,2304]{1,0:T(8,128)(2,1)}, u32[]{:S(2)}) copy-start(bf16[24,2304]{1,0:T(8,128)(2,1)} %param.28) | copy-start | bytes 331780
  412.7 9.3 %copy-start.82 = (bf16[24]{0:T(256)(128)(2,1)S(1)}, bf16[24]{0:T(256)(128)(2,1)}, u32[]{:S(2)}) copy-start(bf16[24]{0:T(256)(128)(2,1)} %param.27) | copy-start | bytes 148
  412.7 9.8 %copy-start.26 = (bf16[128,768]{1,0:T(8,128)(2,1)S(1)}, bf16[128,768]{1,0:T(8,128)(2,1)}, u32[]{:S(2)}) copy-start(bf16[128,768]{1,0:T(8,128)(2,1)} %refs_13_.1) | copy-start | bytes 589828
  412.7 9.8 %copy-start.30 = (bf16[12,64,128]{2,1,0:T(8,128)(2,1)S(1)}, bf16[12,64,128]{2,1,0:T(8,128)(2,1)}, u32[]{:S(2)}) copy-start(bf16[12,64,128]{2,1,0:T(8,128)(2,1)} %copy-done.29) | copy-start | bytes 589828
  412.8 9.8 %copy-start.56 = (bf16[12,64,128]{2,1,0:T(8,128)(2,1)S(1)}, bf16[12,64,128]{2,1,0:T(8,128)(2,1)}, u32[]{:S(2)}) copy-start(bf16[12,64,128]{2,1,0:T(8,128)(2,1)} %convolution_convert_fusion.15) | copy-start | bytes 589828
  412.8 9.8 %copy-start.57 = (bf16[12,64,128]{2,1,0:T(8,128)(2,1)S(1)}, bf16[12,64,128]{2,1,0:T(8,128)(2,1)}, u32[]{:S(2)}) copy-start(bf16[12,64,128]{2,1,0:T(8,128)(2,1)} %convolution_convert_fusion.14) | copy-start | bytes 589828
  412.8 9.8 %copy-start.74 = (f32[768]{0:T(1024)S(1)}, f32[768]{0:T(1024)}, u32[]{:S(2)}) copy-start(f32[768]{0:T(1024)} %get-tuple-element.125) | copy-start | bytes 9220
  422.6 4.6 %copy-start.9 = (bf16[256,768]{1,0:T(8,128)(2,1)S(1)}, bf16[256,768]{1,0:T(8,128)(2,1)}, u32[]{:S(2)}) copy-start(bf16[256,768]{1,0:T(8,128)(2,1)} %refs_12_.1) | copy-start | bytes 1179652
  422.6 4.5 %copy-start.73 = (f32[768]{0:T(1024)S(1)}, f32[768]{0:T(1024)}, u32[]{:S(2)}) copy-start(f32[768]{0:T(1024)} %get-tuple-element.127) | copy-start | bytes 9220
  422.6 4.5 %copy-start.83 = (bf16[4,2,2,2,3,8,2304]{6,5,4,3,2,1,0:T(8,128)(2,1)S(1)}, bf16[4,2,2,2,3,8,2304]{6,5,4,3,2,1,0:T(8,128)(2,1)}, u32[]{:S(2)}) copy-start(bf16[4,2,2,2,3,8,2304]{6,5,4,3,2,1,0:T(8,128)(2,1)} %get-tuple-element.85) | copy-start | bytes 10616836
  422.6 4.5 %copy-start.88 = (bf16[12,64,256]{2,1,0:T(8,128)(2,1)S(1)}, bf16[12,64,256]{2,1,0:T(8,128)(2,1)}, u32[]{:S(2)}) copy-start(bf16[12,64,256]{2,1,0:T(8,128)(2,1)} %fusion.43) | copy-start | bytes 1179652
  422.6 4.5 %copy-start.90 = (bf16[12,64,256]{2,1,0:T(8,128)(2,1)S(1)}, bf16[12,64,256]{2,1,0:T(8,128)(2,1)}, u32[]{:S(2)}) copy-start(bf16[12,64,256]{2,1,0:T(8,128)(2,1)} %fusion.46) | copy-start | bytes 1179652
  422.6 4.5 %copy-start.92 = (bf16[12,64,256]{2,1,0:T(8,128)(2,1)S(1)}, bf16[12,64,256]{2,1,0:T(8,128)(2,1)}, u32[]{:S(2)}) copy-start(bf16[12,64,256]{2,1,0:T(8,128)(2,1)} %copy-done.91) | copy-start | bytes 1179652
  428.5 3.3 copy-start.61
  428.5 3.9 copy-start.11
  428.5 4.7 %copy-start.52 = (f32[8,8,768]{2,1,0:T(8,128)S(1)}, f32[8,8,768]{2,1,0:T(8,128)}, u32[]{:S(2)}) copy-start(f32[8,8,768]{2,1,0:T(8,128)} %get-tuple-element.105) | copy-start | bytes 589828
  429.6 4.2 copy-start.19
  429.6 4.9 %copy-start.60 = (f32[3,8,768]{2,1,0:T(8,128)S(1)}, f32[3,8,768]{2,1,0:T(8,128)}, u32[]{:S(2)}) copy-start(f32[3,8,768]{2,1,0:T(8,128)} %get-tuple-element.107) | copy-start | bytes 221188
  429.6 5.5 %copy-start.47 = (f32[3,8,768]{2,1,0:T(8,128)S(1)}, f32[3,8,768]{2,1,0:T(8,128)}, u32[]{:S(2)}) copy-start(f32[3,8,768]{2,1,0:T(8,128)} %get-tuple-element.108) | copy-start | bytes 221188
  429.6 6.2 %copy-start.33 = (f32[3,8,1536]{2,1,0:T(8,128)S(1)}, f32[3,8,1536]{2,1,0:T(8,128)}, u32[]{:S(2)}) copy-start(f32[3,8,1536]{2,1,0:T(8,128)} %get-tuple-element.109) | copy-start | bytes 442372
  429.6 6.8 %copy-start.59 = (f32[3,8,768]{2,1,0:T(8,128)S(1)}, f32[3,8,768]{2,1,0:T(8,128)}, u32[]{:S(2)}) copy-start(f32[3,8,768]{2,1,0:T(8,128)} %get-tuple-element.110) | copy-start | bytes 221188
  429.6 7.5 %copy-start.10 = (f32[3,8,4096]{2,1,0:T(8,128)S(1)}, f32[3,8,4096]{2,1,0:T(8,128)}, u32[]{:S(2)}) copy-start(f32[3,8,4096]{2,1,0:T(8,128)} %get-tuple-element.111) | copy-start | bytes 1179652
  430.4 7.4 %copy-start.50 = (f32[8,8,768]{2,1,0:T(8,128)S(1)}, f32[8,8,768]{2,1,0:T(8,128)}, u32[]{:S(2)}) copy-start(f32[8,8,768]{2,1,0:T(8,128)} %get-tuple-element.112) | copy-start | bytes 589828
  (33 other events, 62.2 us)
